TPU v7x, 512 devices: a whole 4x4x16 slice. The times are simulated.
512 devices in a mesh: prompt: 16 (over x, y_hi, core), branch: 32 (over z, y_lo).
Axes of the slice: x: 4, y: 4 (y_hi: 2, y_lo: 2; y = y_hi * 2 + y_lo), z: 16, core: 2. Of those that a mesh axis runs over, the one named last changes fastest.
Arguments:
- queries: bfloat16 [16, 32, 256, 1024], P('prompt', 'branch'), may hold values from -8 to 8
- resp_keys: bfloat16 [16, 32, 256, 128], P('prompt', 'branch'), may hold values from -6 to 6
- resp_values: bfloat16 [16, 32, 256, 128], P('prompt', 'branch'), may hold values from -6 to 6
- trunk_keys: bfloat16 [16, 1024, 128], P('prompt', 'branch'), may hold values from -8 to 8
- trunk_values: bfloat16 [16, 1024, 128], P('prompt', 'branch'), may hold values from -6 to 6
- header_keys: bfloat16 [512, 128], P('prompt'), may hold values from -6 to 6
- header_values: bfloat16 [512, 128], P('prompt'), may hold values from -6 to 6
- out_grad: bfloat16 [16, 32, 256, 1024], P('prompt', 'branch'), may hold values from -96 to 96
- lengths: int32 [16, 32], P('prompt', 'branch'), may hold values from 64 to 256, as said below
- forks: int32 [16, 32], P('prompt', 'branch'), may hold values from 1 to 8, as said below
Outputs:
- query_grad: bfloat16 [16, 32, 256, 1024], P('prompt', 'branch')
- resp_key_grad: bfloat16 [16, 32, 256, 128], P('prompt', 'branch')
- resp_value_grad: bfloat16 [16, 32, 256, 128], P('prompt', 'branch')
- trunk_key_grad: float32 [16, 1024, 128], P('prompt', 'branch')
- trunk_value_grad: float32 [16, 1024, 128], P('prompt', 'branch')
- header_key_grad: float32 [512, 128], P('prompt')
- header_value_grad: float32 [512, 128], P('prompt')
Inputs may be any that keep to these rules, and one draw needn't show every extreme that they name: `lengths`: every prompt has one response of exactly 256 live tokens. `forks`: every prompt has one response that sees all 8 trunk blocks.
All inputs are finite; a program needn't handle non-finite values.
Results may differ from a plain program's by a relative error of at most 0.0087.
Values may be sent and summed in bfloat16 or wider, within the bound.
A program may use at most 64 MiB of HBM per device.

v0:
```python
import jax
import jax.numpy as jnp
from jax import lax
from jax.sharding import PartitionSpec as P

DH = 128
H = 8
BLK = 128


MASKED_SCORE = -1e30


def visible_mask(block_start, span_width, query_pos, head_len, trunk_len, fork_depth):
    column = block_start + jnp.arange(span_width, dtype=jnp.int32)[None, :]
    in_head = column < head_len
    in_trunk = (
        (column >= head_len)
        & (column < head_len + trunk_len)
        & ((column - head_len) // BLK < fork_depth)
    )
    in_resp = (column >= head_len + trunk_len) & (
        column - head_len - trunk_len <= query_pos[:, None]
    )
    return in_head | in_trunk | in_resp


def per_device(
    queries,
    resp_keys,
    resp_values,
    trunk_keys,
    trunk_values,
    header_keys,
    header_values,
    out_grad,
    lengths,
    forks,
):
    trunk_k, trunk_v = (
        lax.all_gather(trunk_keys, "branch", axis=1, tiled=True),
        lax.all_gather(trunk_values, "branch", axis=1, tiled=True),
    )
    head_k, head_v = (
        lax.all_gather(header_keys, "prompt", axis=0, tiled=True),
        lax.all_gather(header_values, "prompt", axis=0, tiled=True),
    )
    head_len = head_k.shape[0]
    trunk_len = trunk_k.shape[1]
    resp_len = queries.shape[2]
    row_count = resp_len * H
    score_scale = DH ** (-0.5)
    fork_depth = forks[0, 0]
    live_rows = jnp.arange(resp_len, dtype=jnp.int32) < lengths[0, 0]
    query_flat = queries[0, 0].reshape(row_count, DH)
    grad_flat = jnp.where(
        live_rows[:, None], out_grad[0, 0], jnp.zeros_like(out_grad[0, 0])
    ).reshape(row_count, DH)
    query_pos = jnp.arange(row_count, dtype=jnp.int32) // H
    all_keys = jnp.concatenate([head_k, trunk_k[0], resp_keys[0, 0]], axis=0)
    all_values = jnp.concatenate([head_v, trunk_v[0], resp_values[0, 0]], axis=0)
    key_total = all_keys.shape[0]
    block_count = key_total // BLK
    key_blocks = all_keys.reshape(block_count, BLK, DH)
    value_blocks = all_values.reshape(block_count, BLK, DH)
    block_starts = jnp.arange(block_count, dtype=jnp.int32) * BLK

    def scores(block_start, key_block):
        raw = jnp.dot(query_flat, key_block.T, preferred_element_type=jnp.float32) * score_scale
        allowed = visible_mask(
            block_start, key_block.shape[0], query_pos, head_len, trunk_len, fork_depth
        )
        return jnp.where(allowed, raw, MASKED_SCORE)

    def forward(carry, block_item):
        running_max, denom_sum, delta_sum = carry
        block_start, key_block, value_block = block_item
        logits = scores(block_start, key_block)
        prob_grad = jnp.dot(grad_flat, value_block.T, preferred_element_type=jnp.float32)
        new_max = jnp.maximum(running_max, jnp.max(logits, axis=1))
        factor = jnp.exp(running_max - new_max)
        exp_terms = jnp.exp(logits - new_max[:, None])
        denom_sum = denom_sum * factor + jnp.sum(exp_terms, axis=1)
        delta_sum = delta_sum * factor + jnp.sum(exp_terms * prob_grad, axis=1)
        return ((new_max, denom_sum, delta_sum), None)

    start_stats = (
        jnp.full((row_count,), MASKED_SCORE, jnp.float32),
        jnp.zeros((row_count,), jnp.float32),
        jnp.zeros((row_count,), jnp.float32),
    )
    final_stats, _ = lax.scan(forward, start_stats, (block_starts, key_blocks, value_blocks))
    running_max, denom_sum, delta_sum = final_stats
    log_total = running_max + jnp.log(denom_sum)
    row_delta = delta_sum / denom_sum

    def block_probs(block_start, key_block, value_block):
        logits = scores(block_start, key_block)
        prob_full = jnp.exp(logits - log_total[:, None])
        prob_grad = jnp.dot(grad_flat, value_block.T, preferred_element_type=jnp.float32)
        score_grad = (prob_full * (prob_grad - row_delta[:, None]) * score_scale).astype(
            jnp.bfloat16
        )
        return (score_grad, prob_full.astype(jnp.bfloat16))

    def key_value_terms(score_grad, prob_low):
        key_term = jnp.einsum(
            "rk,rd->kd", score_grad, query_flat, preferred_element_type=jnp.float32
        )
        value_term = jnp.einsum(
            "rk,rd->kd", prob_low, grad_flat, preferred_element_type=jnp.float32
        )
        return jnp.concatenate([key_term, value_term], axis=1)

    def backward_full(query_acc, block_item):
        block_start, key_block, value_block = block_item
        score_grad, prob_low = block_probs(block_start, key_block, value_block)
        query_acc = query_acc + jnp.dot(score_grad, key_block, preferred_element_type=jnp.float32)
        return (query_acc, key_value_terms(score_grad, prob_low))

    init_grad = jnp.zeros((row_count, DH), jnp.float32)
    query_acc, all_terms = lax.scan(
        backward_full, init_grad, (block_starts, key_blocks, value_blocks)
    )
    all_terms = all_terms.reshape(key_total, 2 * DH)
    head_term = all_terms[:head_len]
    resp_term = all_terms[head_len + trunk_len :]
    trunk_owned = lax.psum_scatter(
        all_terms[head_len : head_len + trunk_len], "branch", scatter_dimension=0, tiled=True
    )
    whole_sum = lax.psum(head_term, "branch")
    head_owned = lax.psum_scatter(whole_sum, "prompt", scatter_dimension=0, tiled=True)
    query_grad = query_acc.astype(jnp.bfloat16).reshape(1, 1, resp_len, H * DH)
    resp_kgrad = resp_term[:, :DH].astype(jnp.bfloat16).reshape(1, 1, resp_len, DH)
    resp_vgrad = resp_term[:, DH:].astype(jnp.bfloat16).reshape(1, 1, resp_len, DH)
    trunk_kgrad = trunk_owned[:, :DH][None]
    trunk_vgrad = trunk_owned[:, DH:][None]
    head_kgrad = head_owned[:, :DH]
    head_vgrad = head_owned[:, DH:]
    return (query_grad, resp_kgrad, resp_vgrad, trunk_kgrad, trunk_vgrad, head_kgrad, head_vgrad)


def solution(mesh):
    placed = (
        P("prompt", "branch", None, None),
        P("prompt", "branch", None, None),
        P("prompt", "branch", None, None),
        P("prompt", "branch", None),
        P("prompt", "branch", None),
        P("prompt", None),
        P("prompt", None),
        P("prompt", "branch", None, None),
        P("prompt", "branch"),
        P("prompt", "branch"),
    )
    return jax.shard_map(
        per_device,
        mesh=mesh,
        in_specs=placed,
        out_specs=(
            P("prompt", "branch", None, None),
            P("prompt", "branch", None, None),
            P("prompt", "branch", None, None),
            P("prompt", "branch", None),
            P("prompt", "branch", None),
            P("prompt", None),
            P("prompt", None),
        ),
        check_vma=False,
    )
```

profile of v0, /device:TPU:6, one launch (start us, length us, event | category | flops | bytes accessed | tf_op | source)
XLA Modules:
  0.0 539.7 jit_solution(3298957861393011590)
XLA Ops:
  8.2 22.1 %all_gather.12 = bf16[512,128]{1,0:T(8,128)(2,1)S(1)} all-gather(bf16[32,128]{1,0:T(8,128)(2,1)} %param.19), channel_id=1, replica_groups=mesh['prompt'=16,'branch'=32] {'prompt'}, dimensions={0}, use_global_device_ids=true | all-gather | bytes 139264 | tf_op jit(solution)/shard_map/all_gather | solution.py:45
  30.3 22.4 %all_gather.14 = bf16[512,128]{1,0:T(8,128)(2,1)S(1)} all-gather(bf16[32,128]{1,0:T(8,128)(2,1)} %param.20), channel_id=1, replica_groups=mesh['prompt'=16,'branch'=32] {'prompt'}, dimensions={0}, use_global_device_ids=true | all-gather | bytes 139264 | tf_op jit(solution)/shard_map/all_gather | solution.py:46
  52.7 66.8 %all_gather.13 = bf16[1,1024,128]{2,1,0:T(8,128)(2,1)S(1)} all-gather(bf16[1,32,128]{2,1,0:T(8,128)(2,1)} %param.17), channel_id=1, replica_groups=mesh['prompt'=16,'branch'=32] {'branch'}, dimensions={1}, use_global_device_ids=true | all-gather | bytes 270336 | tf_op jit(solution)/shard_map/all_gather | solution.py:41
  119.5 60.0 %all_gather.15 = bf16[1,1024,128]{2,1,0:T(8,128)(2,1)S(1)} all-gather(bf16[1,32,128]{2,1,0:T(8,128)(2,1)} %param.18), channel_id=1, replica_groups=mesh['prompt'=16,'branch'=32] {'branch'}, dimensions={1}, use_global_device_ids=true | all-gather | bytes 270336 | tf_op jit(solution)/shard_map/all_gather | solution.py:42
  182.0 49.8 %while.36 = (s32[]{:T(128)}, f32[2048]{0:T(1024)S(1)}, f32[2048]{0:T(1024)S(1)}, f32[2048]{0:T(1024)S(1)}, s32[14]{0:T(128)S(1)}, /*index=5*/s32[]{:T(128)}, bf1...) while((s32[]{:T(128)}, f32[2048]{0:T(1024)S(1)}, ...), condition=%wide.region_4.5_spmd.clone, body=%wide.region_0.4_spmd.clone.sunk | while | flops 137135488 | bytes 4426152 | solution.py:92
  183.2 1.3 and_or_fusion.4
  186.8 1.3 and_or_fusion.4
  190.3 1.3 and_or_fusion.4
  193.9 1.3 and_or_fusion.4
  197.5 1.3 and_or_fusion.4
  201.0 1.3 and_or_fusion.4
  204.6 1.3 and_or_fusion.4
  208.1 1.3 and_or_fusion.4
  211.7 1.3 and_or_fusion.4
  215.2 1.3 and_or_fusion.4
  218.8 1.3 and_or_fusion.4
  222.3 1.3 and_or_fusion.4
  225.9 1.3 and_or_fusion.4
  229.4 1.3 and_or_fusion.4
  231.8 73.0 %while.37 = (s32[]{:T(128)}, f32[2048,128]{1,0:T(8,128)S(1)}, f32[14,128,256]{1,2,0:T(8,128)}, s32[14]{0:T(128)S(1)}, s32[]{:T(128)}, /*index=5*/bf16[14,128,128...) while((s32[]{:T(128)}, f32[2048,128]{1,0:T(8,128)S(1)}, ...), condition=%wide.region_6.7_spmd.clone, body=%wide.region_5.6_spmd.clone.sunk | while | flops 339004800 | bytes 9439671 | solution.py:122
  233.0 1.3 and_or_fusion.5
  238.2 1.3 and_or_fusion.5
  259.1 1.3 and_or_fusion.5
  264.3 1.3 and_or_fusion.5
  285.1 1.3 and_or_fusion.5
  295.5 1.3 and_or_fusion.5
  300.7 1.3 and_or_fusion.5
  308.2 1.3 copy.21
  312.4 80.1 %reduce-scatter.5.cloned.1.call-done = f32[32,256]{1,0:T(8,128)} async-done(((f32[512,256]{1,0:T(8,128)}), f32[32,256]{1,0:T(8,128)}) %reduce-scatter.5.cloned.1.call-update) | async-done | bytes 32784 | tf_op jit(solution)/shard_map/reduce_scatter | solution.py:132
  392.5 122.5 %psum.8 = f32[32,256]{1,0:T(8,128)S(1)} all-reduce(f32[32,256]{1,0:T(8,128)} %reduce-scatter.5.cloned.1.call-done), channel_id=1, replica_groups=mesh['prompt'=16,'branch'=32] {'branch'}, use_global_device_ids=true, to_apply=%region_8.9 | all-reduce | flops 8192 | bytes 65536 | tf_op jit(solution)/shard_map/psum | solution.py:131
  515.7 15.8 %reduce-scatter.3.cloned.1.call-done = f32[32,256]{1,0:T(8,128)} async-done(((f32[1024,256]{1,0:T(8,128)}), f32[32,256]{1,0:T(8,128)}) %reduce-scatter.3.cloned.1.call-update) | async-done | bytes 32784 | tf_op jit(solution)/shard_map/reduce_scatter | solution.py:128
  531.5 1.3 slice_bitcast_fusion.2
  (293 shorter events, 102.9 us)
Async XLA Ops:
  7.2 173.7 %copy-start = (bf16[1,1,256,1024]{3,2,1,0:T(8,128)(2,1)S(1)}, bf16[1,1,256,1024]{3,2,1,0:T(8,128)(2,1)}, u32[]{:S(2)}) copy-start(bf16[1,1,256,1024]{3,2,1,0:T(8,128)(2,1)} %param.21) | copy-start | bytes 1572868
  7.2 385.4 %reduce-scatter.5.cloned.1.call-start = ((), (), s32[]{:S(2)}) async-start(), calls=%async_computation.3 | async-start | bytes 557056 | tf_op jit(solution)/shard_map/reduce_scatter | solution.py:132
  52.7 128.8 %copy-start.1 = (bf16[1,1,256,128]{3,2,1,0:T(8,128)(2,1)S(1)}, bf16[1,1,256,128]{3,2,1,0:T(8,128)(2,1)}, u32[]{:S(2)}) copy-start(bf16[1,1,256,128]{3,2,1,0:T(8,128)(2,1)} %param.15) | copy-start | bytes 196612
  181.1 0.8 copy-start.2
  306.8 224.6 %reduce-scatter.3.cloned.1.call-start = ((), (), s32[]{:S(2)}) async-start(), calls=%async_computation.2 | async-start | bytes 1081344 | tf_op jit(solution)/shard_map/reduce_scatter | solution.py:128
Sparse Core Ops, SparseCore 0:
  307.0 85.5 reduce-scatter.4
  395.5 135.8 reduce-scatter.2
where the time goes:
time: 541 us; the launch traced here: 540 us
  blocking collectives  294 us (54%)
  waiting for transfers between devices  96 us (18%)
  other arithmetic  67.2 us (12%)
  matrix products  37.7 us (7%)
  local copies, waits for them, and re-layouts  28 us (5%)
  between operations  14.9 us (3%)
    psum x1, blocking collectives, per_device(): whole_sum = lax.psum(head_term, 'branch')  123 us
    reduce_scatter x1, waiting for transfers between devices, per_device(): lax.psum_scatter(whole_sum, 'prompt', scatter_dimension=0, tiled=True)  80.1 us
    all_gather x1, blocking collectives, per_device(): lax.all_gather(trunk_keys, 'branch', axis=1, tiled=True)  66.8 us
    all_gather x1, blocking collectives, per_device(): lax.all_gather(trunk_values, 'branch', axis=1, tiled=True)  60 us
    or x28, other arithmetic, visible_mask(): return in_head | in_trunk | in_resp  36.7 us
    all_gather x1, blocking collectives, per_device(): lax.all_gather(header_values, 'prompt', axis=0, tiled=True)  22.4 us
    all_gather x1, blocking collectives, per_device(): lax.all_gather(header_keys, 'prompt', axis=0, tiled=True)  22.1 us
    sub x28, other arithmetic, visible_mask(): column - head_len - trunk_len <= query_pos[:, None]  18.1 us
  transfers between devices with their start and end apart: 2, of which 2 were waited for; matrix products, arithmetic and copies ran while one was open for 1% of the time, Pallas kernels for 0%

commit v1 on v0

v1 whole, which is shorter than its diff:
```python
import functools

import jax
import jax.numpy as jnp
from jax import lax
from jax.experimental import pallas as pl
from jax.experimental.pallas import tpu as pltpu
from jax.sharding import PartitionSpec as P

DH = 128
H = 8
BLK = 128
RESP = 256
HDR = 512
PREF = 1024
NP = 16
NB = 32
NZ = 16
CH = 256
KEYS = HDR + PREF + RESP
NCH = KEYS // CH
FAR = 5
NEAR = (-2, -1, 1, 2)
LOW = -1e30
SCALE = DH**-0.5
LOG2E = 1.4426950408889634
C2 = SCALE * LOG2E
MESH = pl.DeviceIdType.MESH
F32 = jnp.float32
BF16 = jnp.bfloat16


def mod(a, n):
    return lax.rem(a + 4 * n, n)


def kernel(
    lengths, forks, q_hbm, rk_hbm, rv_hbm, tk_hbm, tv_hbm, hk_hbm, hv_hbm, g_hbm,
    dq_out, rkg_out, rvg_out, tkg_out, tvg_out, hkg_out, hvg_out,
    qf, gf, qt, gt, ka, va, kt, hkv, tkv, e_s, dp_s, ds_s, m_s, l_s, d_s, mb_s, fac_s, del_s,
    tb, r1, ra, cs, r2, hb, rh, zs, rz, ro, rg,
    in_sem, own_sem, gs, hrs, trs, ars, s1, q1, qa, s2, q2, sh, qh, sz, qz, sg, qg,
):
    p = lax.axis_index("prompt")
    b = lax.axis_index("branch")
    z = b // 2
    y = lax.rem(b, 2)
    yo = 1 - y
    plane = p * 2 + y

    def at(dz, yy):
        return mod(z + dz, NZ) * 2 + yy

    barrier = pltpu.get_barrier_semaphore()
    greet = [(p, at(s * FAR, yy)) for s in (-1, 1) for yy in (y, yo)]
    greet += [(p, at(j, yy)) for j in (-3, -2, -1, 1, 2, 3) for yy in (y, yo)]
    greet += [(p, at(0, yo))]
    greet += [(mod(p + o, NP), b) for o in range(1, NP)]
    for d in greet:
        pl.semaphore_signal(barrier, 1, device_id=d, device_id_type=MESH)

    own = [
        pltpu.make_async_copy(hk_hbm, hkv.at[p, pl.ds(0, 32)], own_sem.at[0]),
        pltpu.make_async_copy(hv_hbm, hkv.at[p, pl.ds(32, 32)], own_sem.at[1]),
        pltpu.make_async_copy(tk_hbm.at[0], tkv.at[b, pl.ds(0, 32)], own_sem.at[2]),
        pltpu.make_async_copy(tv_hbm.at[0], tkv.at[b, pl.ds(32, 32)], own_sem.at[3]),
    ]
    for c in own:
        c.start()
    loads = [
        pltpu.make_async_copy(rk_hbm.at[0, 0], ka.at[pl.ds(HDR + PREF, RESP)], in_sem.at[0]),
        pltpu.make_async_copy(rv_hbm.at[0, 0], va.at[pl.ds(HDR + PREF, RESP)], in_sem.at[1]),
    ]
    for h in range(H):
        loads.append(pltpu.make_async_copy(
            q_hbm.at[0, 0, :, pl.ds(h * DH, DH)], qf.at[pl.ds(h * RESP, RESP)], in_sem.at[2 + h]))
        loads.append(pltpu.make_async_copy(
            g_hbm.at[0, 0, :, pl.ds(h * DH, DH)], gf.at[pl.ds(h * RESP, RESP)], in_sem.at[2 + H + h]))
    for c in loads:
        c.start()

    for c in own:
        c.wait()
    pl.semaphore_wait(barrier, len(greet))

    sent = []

    def send(src, dst, ssem, rsem, dev):
        c = pltpu.make_async_remote_copy(
            src_ref=src, dst_ref=dst, send_sem=ssem, recv_sem=rsem, device_id=dev, device_id_type=MESH)
        c.start()
        sent.append(c)

    n = 0
    slots = [b, at(-FAR, y), at(FAR, y)]
    for s in (-1, 1):
        send(tkv.at[b], tkv.at[b], gs.at[n], trs.at[b], (p, at(s * FAR, y)))
        n += 1
    near = [at(j, yy) for j in NEAR for yy in (y, yo)] + [at(0, yo)]
    for d in near:
        send(tkv.at[b], tkv.at[b], gs.at[n], trs.at[b], (p, d))
        n += 1
    for o in range(1, NP):
        send(hkv.at[p], hkv.at[p], gs.at[n], hrs.at[p], (mod(p + o, NP), b))
        n += 1

    for c in loads:
        c.wait()
    live = lax.broadcasted_iota(jnp.int32, (RESP, DH), 0) < lengths[0, 0]

    def prepare(h, _):
        rows = pl.ds(pl.multiple_of(h * RESP, RESP), RESP)
        g = jnp.where(live, gf[rows, :], jnp.zeros((), BF16))
        gf[rows, :] = g
        gt[h] = g.T
        qt[h] = qf[rows, :].T
        m_s[h] = jnp.full((1, RESP), LOW, F32)
        l_s[h] = jnp.zeros((8, RESP), F32)
        d_s[h] = jnp.zeros((8, RESP), F32)
        return 0

    lax.fori_loop(0, H, prepare, 0)
    fork = forks[0, 0]

    def stats(i, h, kind):
        rows = pl.ds(i * CH if isinstance(i, int) else pl.multiple_of(i * CH, CH), CH)
        s = jnp.dot(ka[rows, :], qt[h], preferred_element_type=F32)
        dp = jnp.dot(va[rows, :], gt[h], preferred_element_type=F32)
        if kind == "resp":
            key = lax.broadcasted_iota(jnp.int32, (CH, RESP), 0)
            pos = lax.broadcasted_iota(jnp.int32, (CH, RESP), 1)
            s = jnp.where(key <= pos, s, LOW)
        m_old = m_s[h]
        halves = []
        m_new = m_old
        for u in range(2):
            top = jnp.max(s[u * BLK : (u + 1) * BLK], axis=0, keepdims=True)
            seen = None
            if kind == "trunk":
                seen = jnp.broadcast_to((i - HDR // CH) * 2 + u, (1, RESP)) < fork
                top = jnp.where(seen, top, LOW)
            halves.append(seen)
            m_new = jnp.maximum(m_new, top)
        f = jnp.exp2((m_old - m_new) * C2)
        shift = m_new * C2
        l = l_s[h] * f
        d = d_s[h] * f
        for u in range(2):
            sh_u = shift if halves[u] is None else jnp.where(halves[u], shift, -LOW)
            e = jnp.exp2(s[u * BLK : (u + 1) * BLK] * C2 - sh_u)
            dpu = dp[u * BLK : (u + 1) * BLK]
            l = l + jnp.sum(e.reshape(BLK // 8, 8, RESP), axis=0)
            d = d + jnp.sum((e * dpu).reshape(BLK // 8, 8, RESP), axis=0)
            r = pl.ds(i * CH + u * BLK if isinstance(i, int) else pl.multiple_of(i * CH + u * BLK, BLK), BLK)
            e_s[h, r, :] = e
            dp_s[h, r, :] = dpu
        l_s[h] = l
        d_s[h] = d
        m_s[h] = m_new
        mb_s[i, h] = m_new

    def stats_of(i, kind):
        def body(h, _):
            stats(i, h, kind)
            return 0
        lax.fori_loop(0, H, body, 0, unroll=2)

    stats_of(NCH - 1, "resp")

    for s in slots[1:]:
        pltpu.make_async_remote_copy(
            src_ref=tkv.at[s], dst_ref=tkv.at[s], send_sem=gs.at[0], recv_sem=trs.at[s],
            device_id=(p, at(1, y)), device_id_type=MESH).wait_recv()
    for s in slots[1:]:
        for d in near:
            send(tkv.at[s], tkv.at[s], gs.at[n], trs.at[s], (p, d))
            n += 1
    kk, vv = pl.ds(0, 32), pl.ds(32, 32)
    for yy in (y, yo):
        send(tkv.at[slots[1], kk], tkv.at[slots[1], kk], gs.at[n], trs.at[slots[1]], (p, at(3, yy)))
        n += 1
        send(tkv.at[slots[2], vv], tkv.at[slots[2], vv], gs.at[n], ars.at[lax.rem(slots[2], 2)], (p, at(-3, yy)))
        n += 1

    def arrived(ref, sem):
        pltpu.make_async_remote_copy(
            src_ref=ref, dst_ref=ref, send_sem=gs.at[0], recv_sem=sem,
            device_id=(p, at(1, y)), device_id_type=MESH).wait_recv()

    for o in range(1, NP):
        s = mod(p + o, NP)
        arrived(hkv.at[s], hrs.at[s])
    for i in range(NP):
        ka[pl.ds(i * 32, 32), :] = hkv[i, :32, :]
        va[pl.ds(i * 32, 32), :] = hkv[i, 32:, :]
    for i in range(HDR // CH):
        stats_of(i, "head")

    for dz in range(-7, 9):
        for yy in (y, yo):
            s = at(dz, yy)
            if dz == 0 and yy is y:
                continue
            if abs(dz) == FAR and yy is y:
                continue
            if dz == 8:
                arrived(tkv.at[s, kk], trs.at[s])
                arrived(tkv.at[s, vv], ars.at[yy])
            else:
                arrived(tkv.at[s], trs.at[s])
    for i in range(NB):
        ka[pl.ds(HDR + i * 32, 32), :] = tkv[i, :32, :]
        va[pl.ds(HDR + i * 32, 32), :] = tkv[i, 32:, :]

    def trunk_stats(i, _):
        stats_of(i, "trunk")
        return 0

    lax.fori_loop(HDR // CH, (HDR + PREF) // CH, trunk_stats, 0)

    def finish(h, _):
        inv = 1.0 / jnp.sum(l_s[h], axis=0, keepdims=True)
        del_s[h] = jnp.sum(d_s[h], axis=0, keepdims=True) * inv
        m = m_s[h]
        for i in range(NCH):
            fac_s[i, h] = jnp.exp2((mb_s[i, h] - m) * C2) * inv
        return 0

    lax.fori_loop(0, H, finish, 0)

    def terms(i):
        rows = pl.ds(i * CH if isinstance(i, int) else pl.multiple_of(i * CH, CH), CH)
        kg = jnp.zeros((CH, DH), F32)
        vg = jnp.zeros((CH, DH), F32)
        for h in range(H):
            pr = e_s[h, rows, :] * fac_s[i, h]
            ds = (pr * (dp_s[h, rows, :] - del_s[h])).astype(BF16)
            ds_s[rows, h * RESP : (h + 1) * RESP] = ds
            kg = kg + jnp.dot(ds, qf[h * RESP : (h + 1) * RESP, :], preferred_element_type=F32)
            vg = vg + jnp.dot(pr.astype(BF16), gf[h * RESP : (h + 1) * RESP, :], preferred_element_type=F32)
        return kg * SCALE, vg

    def head_terms(i, _):
        kg, vg = terms(i)
        kg, vg = kg.astype(BF16), vg.astype(BF16)
        for u in range(CH // 16):
            hb[i * (CH // 16) + u, :16, :] = kg[u * 16 : (u + 1) * 16]
            hb[i * (CH // 16) + u, 16:, :] = vg[u * 16 : (u + 1) * 16]
        return 0

    lax.fori_loop(0, HDR // CH, head_terms, 0)

    n = 0
    for o in range(1, 2 * NP):
        d = mod(plane + o, 2 * NP)
        send(hb.at[d], rh.at[plane], sh.at[n], qh.at[plane], (d // 2, z * 2 + lax.rem(d, 2)))
        n += 1

    def trunk_terms(i, _):
        kg, vg = terms(i)
        kg, vg = kg.astype(BF16), vg.astype(BF16)
        for u in range(CH // 32):
            k = (i - HDR // CH) * (CH // 32) + u
            tb[k, :32, :] = kg[u * 32 : (u + 1) * 32]
            tb[k, 32:, :] = vg[u * 32 : (u + 1) * 32]
        return 0

    lax.fori_loop(HDR // CH, (HDR + PREF) // CH, trunk_terms, 0)

    n = 0
    for jn, j in enumerate(NEAR):
        for f in range(3):
            zd = mod(z + j + (f - 1) * FAR, NZ)
            send(tb.at[pl.ds(2 * zd, 2)], r1.at[jn, f], s1.at[n], q1.at[jn, f], (p, at(j, y)))
            n += 1
    anti = mod(z + 8, NZ)
    send(tb.at[pl.ds(2 * anti, 2), kk], ra.at[0], s1.at[n], qa.at[0], (p, at(3, y)))
    n += 1
    send(tb.at[pl.ds(2 * anti, 2), vv], ra.at[1], s1.at[n], qa.at[1], (p, at(-3, y)))

    kg, vg = terms(NCH - 1)
    rkg_out[0, 0] = kg.astype(BF16)
    rvg_out[0, 0] = vg.astype(BF16)

    for o in range(1, 2 * NP):
        s = mod(plane + o, 2 * NP)
        arrived(rh.at[s], qh.at[s])
    rh[plane] = hb[plane]
    acc = jnp.zeros((32, DH), F32)
    for i in range(2 * NP):
        acc = acc + rh[i].astype(F32)
    for i in range(NZ):
        zs[i, 0:1, :] = acc[i : i + 1]
        zs[i, 1:2, :] = acc[16 + i : 17 + i]
    n = 0
    for o in (8, 7, 9, 6, 10, 5, 11, 4, 12, 3, 13, 2, 14, 1, 15):
        d = mod(z + o, NZ)
        send(zs.at[d], rz.at[z], sz.at[n], qz.at[z], (p, d * 2 + y))
        n += 1

    for jn in range(4):
        for f in range(3):
            arrived(r1.at[jn, f], q1.at[jn, f])
    arrived(ra.at[0], qa.at[0])
    arrived(ra.at[1], qa.at[1])
    n = 0
    for f in (0, 2, 1):
        zd = mod(z + (f - 1) * FAR, NZ)
        total = tb[pl.ds(2 * zd, 2)].astype(F32)
        for jn in range(4):
            total = total + r1[jn, f].astype(F32)
        low, high = total[:, :32], total[:, 32:]
        if f == 2:
            low = low + ra[0].astype(F32)
        if f == 0:
            high = high + ra[1].astype(F32)
        cs[f, :, :32] = low.astype(BF16)
        cs[f, :, 32:] = high.astype(BF16)
        if f != 1:
            for w, yy in enumerate((y, yo)):
                send(cs.at[f, yy], r2.at[f, w], s2.at[n], q2.at[f, w], (p, zd * 2 + yy))
                n += 1
        else:
            send(cs.at[f, yo], r2.at[f, 1], s2.at[n], q2.at[f, 1], (p, at(0, yo)))
            n += 1

    for o in range(1, NZ):
        s = mod(z + o, NZ)
        arrived(rz.at[s], qz.at[s])
    rz[z] = zs[z]
    one = rz[0]
    for i in range(1, NZ):
        one = one + rz[i]
    ro[...] = one
    rg[b] = one
    n = 0
    for o in (16, 15, 17, 14, 18, 13, 19, 12, 20, 11, 21, 10, 22, 9, 23, 8, 24, 7, 25, 6, 26, 5, 27, 4, 28, 3, 29, 2, 30, 1, 31):
        d = mod(b + o, NB)
        send(ro, rg.at[b], sg.at[n], qg.at[b], (p, d))
        n += 1

    kt[...] = ka[...].T

    def query_grad(h, _):
        cols = pl.ds(pl.multiple_of(h * RESP, RESP), RESP)
        acc = jnp.dot(kt[...], ds_s[:, cols], preferred_element_type=F32)
        dq_out[0, 0, :, pl.ds(pl.multiple_of(h * DH, DH), DH)] = (acc * SCALE).T.astype(BF16)
        return 0

    lax.fori_loop(0, H, query_grad, 0)

    for f in range(3):
        for w in range(2):
            if f == 1 and w == 0:
                continue
            arrived(r2.at[f, w], q2.at[f, w])
    total = cs[1, y].astype(F32) + r2[1, 1].astype(F32)
    for f in (0, 2):
        for w in range(2):
            total = total + r2[f, w].astype(F32)
    tkg_out[0] = total[:32]
    tvg_out[0] = total[32:]

    for o in range(1, NB):
        s = mod(b + o, NB)
        arrived(rg.at[s], qg.at[s])
    for i in range(32):
        s = (i % NZ) * 2 + i // NZ
        hkg_out[i : i + 1, :] = rg[s, 0:1, :]
        hvg_out[i : i + 1, :] = rg[s, 1:2, :]
    for c in sent:
        c.wait_send()


def per_device(q, rk, rv, tk, tv, hk, hv, g, lengths, forks):
    vm = pl.BlockSpec(memory_space=pltpu.VMEM)
    hbm = pl.BlockSpec(memory_space=pl.ANY)
    smem = pl.BlockSpec(memory_space=pltpu.SMEM)
    dma = pltpu.SemaphoreType.DMA
    sds = jax.ShapeDtypeStruct
    V = pltpu.VMEM
    return pl.pallas_call(
        kernel,
        out_shape=(
            sds((1, 1, RESP, H * DH), BF16), sds((1, 1, RESP, DH), BF16), sds((1, 1, RESP, DH), BF16),
            sds((1, 32, DH), F32), sds((1, 32, DH), F32), sds((32, DH), F32), sds((32, DH), F32),
        ),
        in_specs=[smem, smem] + [hbm] * 8,
        out_specs=(vm,) * 7,
        scratch_shapes=[
            V((H * RESP, DH), BF16), V((H * RESP, DH), BF16),
            V((H, DH, RESP), BF16), V((H, DH, RESP), BF16),
            V((KEYS, DH), BF16), V((KEYS, DH), BF16), V((DH, KEYS), BF16),
            V((NP, 64, DH), BF16), V((NB, 64, DH), BF16),
            V((H, KEYS, RESP), F32), V((H, KEYS, RESP), F32), V((KEYS, H * RESP), BF16),
            V((H, 1, RESP), F32), V((H, 8, RESP), F32), V((H, 8, RESP), F32),
            V((NCH, H, 1, RESP), F32), V((NCH, H, 1, RESP), F32), V((H, 1, RESP), F32),
            V((NB, 64, DH), BF16), V((4, 3, 2, 64, DH), BF16), V((2, 2, 32, DH), BF16),
            V((3, 2, 64, DH), BF16), V((3, 2, 64, DH), BF16),
            V((2 * NP, 32, DH), BF16), V((2 * NP, 32, DH), BF16),
            V((NZ, 2, DH), F32), V((NZ, 2, DH), F32), V((2, DH), F32), V((NB, 2, DH), F32),
            dma((2 + 2 * H,)), dma((4,)),
            dma((48,)), dma((NP,)), dma((NB,)), dma((2,)),
            dma((14,)), dma((4, 3)), dma((2,)),
            dma((5,)), dma((3, 2)),
            dma((31,)), dma((32,)), dma((15,)), dma((NZ,)), dma((31,)), dma((NB,)),
        ],
        compiler_params=pltpu.CompilerParams(
            collective_id=0, has_side_effects=True, vmem_limit_bytes=52 << 20),
    )(lengths, forks, q, rk, rv, tk, tv, hk, hv, g)


def solution(mesh):
    four, three, two = P("prompt", "branch", None, None), P("prompt", "branch", None), P("prompt", None)
    both = P("prompt", "branch")
    return jax.shard_map(
        per_device,
        mesh=mesh,
        in_specs=(four, four, four, three, three, two, two, four, both, both),
        out_specs=(four, four, four, three, three, two, two),
        check_vma=False,
    )
```

time: 541 us -> 76.6 us (0.14)
  the two profiles are of different devices: /device:TPU:6 before, /device:TPU:32 now
where the time goes in v1:
time: 76.6 us; the launch traced here: 76.1 us
  Pallas kernels  63.1 us (82%)
  local copies, waits for them, and re-layouts  11 us (14%)
  between operations  1.95 us (3%)
    pallas_call x1, Pallas kernels, per_device(): pl.pallas_call(kernel, out_shape=(sds((1, 1, RESP, H * DH), BF16), sds((1...  63.1 us
    unnamed x23, local copies, waits for them, and re-layouts  11 us

profile of v1, /device:TPU:32, one launch (start us, length us, event | category | flops | bytes accessed | tf_op | source)
XLA Modules:
  0.0 76.1 jit_solution(13072829965366330579)
XLA Ops:
  1.9 0.0 copy-start
  1.9 1.0 %copy-done = bf16[1,1,256,1024]{3,2,1,0:T(8,128)(2,1)S(1)} copy-done((bf16[1,1,256,1024]{3,2,1,0:T(8,128)(2,1)S(1)}, bf16[1,1,256,1024]{3,2,1,0:T(8,128)(2,1)}, u32[]{:S(2)}) %copy-start) | copy-done | bytes 524312
  3.0 0.0 copy-start.1
  3.0 1.0 %copy-done.1 = bf16[1,1,256,1024]{3,2,1,0:T(8,128)(2,1)S(1)} copy-done((bf16[1,1,256,1024]{3,2,1,0:T(8,128)(2,1)S(1)}, bf16[1,1,256,1024]{3,2,1,0:T(8,128)(2,1)}, u32[]{:S(2)}) %copy-start.1) | copy-done | bytes 524312
  4.0 0.0 copy-start.2
  4.0 0.8 %copy-done.2 = bf16[1,1,256,128]{3,2,1,0:T(8,128)(2,1)S(1)} copy-done((bf16[1,1,256,128]{3,2,1,0:T(8,128)(2,1)S(1)}, bf16[1,1,256,128]{3,2,1,0:T(8,128)(2,1)}, u32[]{:S(2)}) %copy-start.2) | copy-done | bytes 65560
  4.9 0.0 copy-start.3
  4.9 0.8 %copy-done.3 = bf16[1,1,256,128]{3,2,1,0:T(8,128)(2,1)S(1)} copy-done((bf16[1,1,256,128]{3,2,1,0:T(8,128)(2,1)S(1)}, bf16[1,1,256,128]{3,2,1,0:T(8,128)(2,1)}, u32[]{:S(2)}) %copy-start.3) | copy-done | bytes 65560
  5.7 0.0 copy-start.4
  5.7 0.7 copy-done.4
  6.4 0.0 copy-start.5
  6.4 0.7 copy-done.5
  7.1 0.0 copy-start.6
  7.1 0.7 copy-done.6
  7.8 0.0 copy-start.7
  7.8 0.7 copy-done.7
  8.5 63.1 %shard_map.153 = (bf16[1,1,256,1024]{3,2,1,0:T(8,128)(2,1)S(1)}, bf16[1,1,256,128]{3,2,1,0:T(8,128)(2,1)S(1)}, bf16[1,1,256,128]{3,2,1,0:T(8,128)(2,1)S(1)}, f32...) custom-call(s32[1,1]{1,0:T(1,128)S(6)} %copy.24.lengths, ...), custom_call_target="tpu_custom_call" | custom-call | tf_op jit(solution)/shard_map/pallas_call | solution.py:382
  71.6 0.8 %copy.26 = bf16[1,1,256,1024]{3,2,1,0:T(8,128)(2,1)} copy(bf16[1,1,256,1024]{3,2,1,0:T(8,128)(2,1)S(1)} %get-tuple-element.14) | data formatting | bytes 1048576
  72.4 0.6 copy.27
  73.1 0.6 copy.28
  73.7 0.6 copy.29
  74.3 0.6 copy.30
  74.9 0.6 copy.31
  75.5 0.6 copy.32
Async XLA Ops:
  1.9 1.0 %copy-start = (bf16[1,1,256,1024]{3,2,1,0:T(8,128)(2,1)S(1)}, bf16[1,1,256,1024]{3,2,1,0:T(8,128)(2,1)}, u32[]{:S(2)}) copy-start(bf16[1,1,256,1024]{3,2,1,0:T(8,128)(2,1)} %q_hbm.1) | copy-start | bytes 1572868
  3.0 1.0 %copy-start.1 = (bf16[1,1,256,1024]{3,2,1,0:T(8,128)(2,1)S(1)}, bf16[1,1,256,1024]{3,2,1,0:T(8,128)(2,1)}, u32[]{:S(2)}) copy-start(bf16[1,1,256,1024]{3,2,1,0:T(8,128)(2,1)} %g_hbm.1) | copy-start | bytes 1572868
  4.0 0.8 %copy-start.2 = (bf16[1,1,256,128]{3,2,1,0:T(8,128)(2,1)S(1)}, bf16[1,1,256,128]{3,2,1,0:T(8,128)(2,1)}, u32[]{:S(2)}) copy-start(bf16[1,1,256,128]{3,2,1,0:T(8,128)(2,1)} %rk_hbm.1) | copy-start | bytes 196612
  4.9 0.8 %copy-start.3 = (bf16[1,1,256,128]{3,2,1,0:T(8,128)(2,1)S(1)}, bf16[1,1,256,128]{3,2,1,0:T(8,128)(2,1)}, u32[]{:S(2)}) copy-start(bf16[1,1,256,128]{3,2,1,0:T(8,128)(2,1)} %rv_hbm.1) | copy-start | bytes 196612
  5.7 0.7 copy-start.4
  6.4 0.7 copy-start.5
  7.1 0.7 copy-start.6
  7.8 0.7 copy-start.7

commit v2 on v1

v2 whole, which is shorter than its diff:
```python
import functools

import jax
import jax.numpy as jnp
from jax import lax
from jax.experimental import pallas as pl
from jax.experimental.pallas import tpu as pltpu
from jax.sharding import PartitionSpec as P

DH = 128
H = 8
BLK = 128
RESP = 256
HDR = 512
PREF = 1024
NP = 16
NB = 32
NZ = 16
CH = 256
KEYS = HDR + PREF + RESP
NCH = KEYS // CH
FAR = 5
NEAR = (-2, -1, 1, 2)
LOW = -1e30
SCALE = DH**-0.5
LOG2E = 1.4426950408889634
C2 = SCALE * LOG2E
UNROLL = 8
MESH = pl.DeviceIdType.MESH
F32 = jnp.float32
BF16 = jnp.bfloat16


def mod(a, n):
    return lax.rem(a + 4 * n, n)


def kernel(
    len_hbm, fork_hbm, q_hbm, rk_hbm, rv_hbm, tk_hbm, tv_hbm, hk_hbm, hv_hbm, g_hbm,
    dq_out, rkg_out, rvg_out, tkg_out, tvg_out, hkg_out, hvg_out,
    qf, gf, qt, gt, ka, va, kt, hkv, tkv, e_s, dp_s, ds_s, m_s, l_s, d_s, mb_s, fac_s, del_s,
    tb, r1, cs, r2, hb, rh, zs, rz, rg,
    lengths, forks, in_sem, own_sem, gs, hrs, trs, ars, s1, q1, s2, q2, sh, qh, sz, qz, sg, qg,
):
    p = lax.axis_index("prompt")
    b = lax.axis_index("branch")
    z = b // 2
    y = lax.rem(b, 2)
    yo = 1 - y
    plane = p * 2 + y

    def at(dz, yy):
        return mod(z + dz, NZ) * 2 + yy

    barrier = pltpu.get_barrier_semaphore()
    greet = [(p, at(s * FAR, yy)) for s in (-1, 1) for yy in (y, yo)]
    greet += [(p, at(j, yy)) for j in (-3, -2, -1, 1, 2, 3) for yy in (y, yo)]
    greet += [(p, at(0, yo))]
    greet += [(mod(p + o, NP), b) for o in range(1, NP)]
    for d in greet:
        pl.semaphore_signal(barrier, 1, device_id=d, device_id_type=MESH)

    own = [
        pltpu.make_async_copy(hk_hbm, hkv.at[p, pl.ds(0, 32)], own_sem.at[0]),
        pltpu.make_async_copy(hv_hbm, hkv.at[p, pl.ds(32, 32)], own_sem.at[1]),
        pltpu.make_async_copy(tk_hbm.at[0], tkv.at[b, pl.ds(0, 32)], own_sem.at[2]),
        pltpu.make_async_copy(tv_hbm.at[0], tkv.at[b, pl.ds(32, 32)], own_sem.at[3]),
    ]
    for c in own:
        c.start()
    loads = [
        pltpu.make_async_copy(rk_hbm.at[0, 0], ka.at[pl.ds(HDR + PREF, RESP)], in_sem.at[0]),
        pltpu.make_async_copy(rv_hbm.at[0, 0], va.at[pl.ds(HDR + PREF, RESP)], in_sem.at[1]),
    ]
    loads.append(pltpu.make_async_copy(len_hbm, lengths, in_sem.at[2 + 2 * H]))
    loads.append(pltpu.make_async_copy(fork_hbm, forks, in_sem.at[3 + 2 * H]))
    for h in range(H):
        loads.append(pltpu.make_async_copy(
            q_hbm.at[0, 0, :, pl.ds(h * DH, DH)], qf.at[pl.ds(h * RESP, RESP)], in_sem.at[2 + h]))
        loads.append(pltpu.make_async_copy(
            g_hbm.at[0, 0, :, pl.ds(h * DH, DH)], gf.at[pl.ds(h * RESP, RESP)], in_sem.at[2 + H + h]))
    for c in loads:
        c.start()

    for c in own:
        c.wait()
    pl.semaphore_wait(barrier, len(greet))

    sent = []

    def send(src, dst, ssem, rsem, dev):
        c = pltpu.make_async_remote_copy(
            src_ref=src, dst_ref=dst, send_sem=ssem, recv_sem=rsem, device_id=dev, device_id_type=MESH)
        c.start()
        sent.append(c)

    n = 0
    slots = [b, at(-FAR, y), at(FAR, y)]
    for s in (-1, 1):
        send(tkv.at[b], tkv.at[b], gs.at[n], trs.at[b], (p, at(s * FAR, y)))
        n += 1
    near = [at(j, yy) for j in NEAR for yy in (y, yo)] + [at(0, yo)]
    for d in near:
        send(tkv.at[b], tkv.at[b], gs.at[n], trs.at[b], (p, d))
        n += 1
    for o in range(1, NP):
        send(hkv.at[p], hkv.at[p], gs.at[n], hrs.at[p], (mod(p + o, NP), b))
        n += 1

    for c in loads:
        c.wait()
    live = lax.broadcasted_iota(jnp.int32, (RESP, DH), 0) < lengths[0, 0]

    def prepare(h, _):
        rows = pl.ds(pl.multiple_of(h * RESP, RESP), RESP)
        g = jnp.where(live, gf[rows, :], jnp.zeros((), BF16))
        gf[rows, :] = g
        gt[h] = g.T
        qt[h] = qf[rows, :].T
        m_s[h] = jnp.full((1, RESP), LOW, F32)
        l_s[h] = jnp.zeros((8, RESP), F32)
        d_s[h] = jnp.zeros((8, RESP), F32)
        return 0

    lax.fori_loop(0, H, prepare, 0)
    r1[4, 0, :, :32, :] = jnp.zeros((2, 32, DH), BF16)
    r1[4, 1] = jnp.zeros((2, 64, DH), BF16)
    r1[4, 2, :, 32:, :] = jnp.zeros((2, 32, DH), BF16)
    fork = forks[0, 0]

    def stats(h, spots, seen, kind):
        keys = [ka[pl.ds(r, c), :] for r, c in spots]
        vals = [va[pl.ds(r, c), :] for r, c in spots]
        keys = keys[0] if len(keys) == 1 else jnp.concatenate(keys, axis=0)
        vals = vals[0] if len(vals) == 1 else jnp.concatenate(vals, axis=0)
        s = jnp.dot(keys, qt[h], preferred_element_type=F32)
        dp = jnp.dot(vals, gt[h], preferred_element_type=F32)
        if kind == "resp":
            key = lax.broadcasted_iota(jnp.int32, s.shape, 0)
            pos = lax.broadcasted_iota(jnp.int32, s.shape, 1)
            s = jnp.where(key <= pos, s, LOW)
        m_old = m_s[h]
        m_new = m_old
        first = 0
        for (r, c), see in zip(spots, seen):
            top = jnp.max(s[first : first + c], axis=0, keepdims=True)
            m_new = jnp.maximum(m_new, top if see is None else jnp.where(see, top, LOW))
            first += c
        f = jnp.exp2((m_old - m_new) * C2)
        shift = m_new * C2
        l = l_s[h] * f
        d = d_s[h] * f
        first = 0
        for (r, c), see in zip(spots, seen):
            move = shift if see is None else jnp.where(see, shift, -LOW)
            e = jnp.exp2(s[first : first + c] * C2 - move)
            dpu = dp[first : first + c]
            l = l + jnp.sum(e.reshape(c // 8, 8, RESP), axis=0)
            d = d + jnp.sum((e * dpu).reshape(c // 8, 8, RESP), axis=0)
            e_s[h, pl.ds(r, c), :] = e
            dp_s[h, pl.ds(r, c), :] = dpu
            first += c
        l_s[h] = l
        d_s[h] = d
        m_s[h] = m_new
        return m_new

    def stats_of(spots, seen, kind, marks):
        def body(h, _):
            m = stats(h, spots, seen, kind)
            for k in marks:
                mb_s[k, h] = m
            return 0
        lax.fori_loop(0, H, body, 0, unroll=UNROLL)

    def trunk_stats(zs_here):
        for zb in zs_here:
            for w in range(2):
                r = pl.ds(pl.multiple_of(HDR + zb * 64 + w * 32, 32), 32)
                ka[r, :] = tkv[2 * zb + w, :32, :]
                va[r, :] = tkv[2 * zb + w, 32:, :]
        spots = [(pl.multiple_of(HDR + zb * 64, 64), 64) for zb in zs_here]
        seen = [jnp.broadcast_to(zb // 2, (1, RESP)) < fork for zb in zs_here]
        stats_of(spots, seen, "trunk", zs_here)

    stats_of([(HDR + PREF, RESP)], [None], "resp", [NZ + 2])

    for s in slots[1:]:
        pltpu.make_async_remote_copy(
            src_ref=tkv.at[s], dst_ref=tkv.at[s], send_sem=gs.at[0], recv_sem=trs.at[s],
            device_id=(p, at(1, y)), device_id_type=MESH).wait_recv()
    for s in slots[1:]:
        for d in near:
            send(tkv.at[s], tkv.at[s], gs.at[n], trs.at[s], (p, d))
            n += 1
    kk, vv = pl.ds(0, 32), pl.ds(32, 32)
    for yy in (y, yo):
        send(tkv.at[slots[1], kk], tkv.at[slots[1], kk], gs.at[n], trs.at[slots[1]], (p, at(3, yy)))
        n += 1
        send(tkv.at[slots[2], vv], tkv.at[slots[2], vv], gs.at[n], ars.at[lax.rem(slots[2], 2)], (p, at(-3, yy)))
        n += 1

    def arrived(ref, sem):
        pltpu.make_async_remote_copy(
            src_ref=ref, dst_ref=ref, send_sem=gs.at[0], recv_sem=sem,
            device_id=(p, at(1, y)), device_id_type=MESH).wait_recv()

    for o in range(1, NP):
        s = mod(p + o, NP)
        arrived(hkv.at[s], hrs.at[s])
    for i in range(NP):
        ka[pl.ds(i * 32, 32), :] = hkv[i, :32, :]
        va[pl.ds(i * 32, 32), :] = hkv[i, 32:, :]

    def head_stats(i, _):
        stats_of([(pl.multiple_of(i * CH, CH), CH)], [None], "head", [NZ + i])
        return 0

    lax.fori_loop(0, HDR // CH, head_stats, 0)

    def group(j):
        return [mod(z + j + f * FAR, NZ) for f in (0, -1, 1)]

    for zb in group(0):
        arrived(tkv.at[2 * zb + yo], trs.at[2 * zb + yo])
    trunk_stats(group(0))

    def near_group(k, _):
        j = ((k + 1) // 2) * (2 * lax.rem(k, 2) - 1)
        for zb in group(j):
            for yy in (y, yo):
                arrived(tkv.at[2 * zb + yy], trs.at[2 * zb + yy])
        trunk_stats(group(j))
        return 0

    lax.fori_loop(1, 5, near_group, 0)
    anti = mod(z + 8, NZ)
    for yy in (y, yo):
        arrived(tkv.at[2 * anti + yy, kk], trs.at[2 * anti + yy])
        arrived(tkv.at[2 * anti + yy, vv], ars.at[yy])
    trunk_stats([anti])

    def finish(h, _):
        inv = 1.0 / jnp.sum(l_s[h], axis=0, keepdims=True)
        del_s[h] = jnp.sum(d_s[h], axis=0, keepdims=True) * inv
        m = m_s[h]
        for i in range(NZ + 3):
            fac_s[i, h] = jnp.exp2((mb_s[i, h] - m) * C2) * inv
        return 0

    lax.fori_loop(0, H, finish, 0)

    def terms(first, marks):
        rows = pl.ds(first, CH)
        c = CH // len(marks)
        kg = jnp.zeros((CH, DH), F32)
        vg = jnp.zeros((CH, DH), F32)
        for h in range(H):
            pr = [e_s[h, pl.ds(first + u * c, c), :] * fac_s[k, h] for u, k in enumerate(marks)]
            pr = pr[0] if len(pr) == 1 else jnp.concatenate(pr, axis=0)
            ds = (pr * (dp_s[h, rows, :] - del_s[h])).astype(BF16)
            ds_s[rows, h * RESP : (h + 1) * RESP] = ds
            kg = kg + jnp.dot(ds, qf[h * RESP : (h + 1) * RESP, :], preferred_element_type=F32)
            vg = vg + jnp.dot(pr.astype(BF16), gf[h * RESP : (h + 1) * RESP, :], preferred_element_type=F32)
        return kg * SCALE, vg

    def head_terms(i, _):
        kg, vg = terms(pl.multiple_of(i * CH, CH), [NZ + i])
        kg, vg = kg.astype(BF16), vg.astype(BF16)
        for u in range(CH // 16):
            hb[i * (CH // 16) + u, :16, :] = kg[u * 16 : (u + 1) * 16]
            hb[i * (CH // 16) + u, 16:, :] = vg[u * 16 : (u + 1) * 16]
        return 0

    lax.fori_loop(0, HDR // CH, head_terms, 0)

    n = 0
    for o in range(1, 2 * NP):
        d = mod(plane + o, 2 * NP)
        send(hb.at[d], rh.at[plane], sh.at[n], qh.at[plane], (d // 2, z * 2 + lax.rem(d, 2)))
        n += 1

    def route(zd):
        o = mod(zd - z, NZ)
        near_it = jnp.logical_or(o <= 2, o >= NZ - 2)
        f = jnp.where(near_it, 1, jnp.where(o <= 8, 2, 0))
        j = jnp.where(o <= 2, o, jnp.where(o <= 8, o - FAR, jnp.where(o <= 13, o - 11, o - NZ)))
        jn = jnp.where(o == 8, 4, jnp.where(j < 0, j + 2, j + 1))
        return o, j, jn, f

    def near_copies(zd):
        o, j, jn, f = route(zd)
        whole = pltpu.make_async_remote_copy(
            src_ref=tb.at[pl.ds(2 * zd, 2)], dst_ref=r1.at[jn, f], send_sem=s1.at[zd], recv_sem=q1.at[jn, f],
            device_id=(p, mod(z + j, NZ) * 2 + y), device_id_type=MESH)
        low = pltpu.make_async_remote_copy(
            src_ref=tb.at[pl.ds(2 * zd, 2), kk], dst_ref=r1.at[4, 2, :, kk], send_sem=s1.at[zd], recv_sem=q1.at[4, 2],
            device_id=(p, at(3, y)), device_id_type=MESH)
        high = pltpu.make_async_remote_copy(
            src_ref=tb.at[pl.ds(2 * zd, 2), vv], dst_ref=r1.at[4, 0, :, vv], send_sem=s1.at[NZ], recv_sem=q1.at[4, 0],
            device_id=(p, at(-3, y)), device_id_type=MESH)
        return jnp.logical_and(o != 8, j != 0), o == 8, whole, low, high

    def trunk_terms(i, _):
        kg, vg = terms(pl.multiple_of(HDR + i * CH, CH), [i * 4 + u for u in range(4)])
        kg, vg = kg.astype(BF16), vg.astype(BF16)
        for u in range(CH // 32):
            k = i * (CH // 32) + u
            tb[k, :32, :] = kg[u * 32 : (u + 1) * 32]
            tb[k, 32:, :] = vg[u * 32 : (u + 1) * 32]
        for u in range(4):
            one, two, whole, low, high = near_copies(i * 4 + u)

            @pl.when(one)
            def _():
                whole.start()

            @pl.when(two)
            def _():
                low.start()
                high.start()
        return 0

    lax.fori_loop(0, PREF // CH, trunk_terms, 0)

    kg, vg = terms(HDR + PREF, [NZ + 2])
    rkg_out[0, 0] = kg.astype(BF16)
    rvg_out[0, 0] = vg.astype(BF16)

    for o in range(1, 2 * NP):
        s = mod(plane + o, 2 * NP)
        arrived(rh.at[s], qh.at[s])
    rh[plane] = hb[plane]
    acc = jnp.zeros((32, DH), F32)
    for i in range(2 * NP):
        acc = acc + rh[i].astype(F32)
    zs[...] = acc.astype(BF16)

    @pl.when(z != 0)
    def _():
        pltpu.make_async_remote_copy(
            src_ref=zs, dst_ref=rz.at[z], send_sem=sz.at[0], recv_sem=qz.at[z],
            device_id=(p, y), device_id_type=MESH).start()

    dests = [mod(z + (f - 1) * FAR, NZ) for f in range(3)]
    ranks = [sum((other < d).astype(jnp.int32) for other in dests) for d in dests]
    for k in range(3):
        f = sum(jnp.where(r == k, i, 0) for i, r in enumerate(ranks))
        zd = mod(z + (f - 1) * FAR, NZ)
        for jn in range(4):
            arrived(r1.at[jn, f], q1.at[jn, f])

        @pl.when(f == 0)
        def _():
            arrived(r1.at[4, 0, :, vv], q1.at[4, 0])

        @pl.when(f == 2)
        def _():
            arrived(r1.at[4, 2, :, kk], q1.at[4, 2])

        total = tb[pl.ds(2 * zd, 2)].astype(F32)
        for jn in range(5):
            total = total + r1[jn, f].astype(F32)
        cs[f] = total.astype(BF16)

        @pl.when(f != 1)
        def _():
            pltpu.make_async_remote_copy(
                src_ref=cs.at[f, y], dst_ref=r2.at[f, 0], send_sem=s2.at[f, 0], recv_sem=q2.at[f, 0],
                device_id=(p, zd * 2 + y), device_id_type=MESH).start()

        pltpu.make_async_remote_copy(
            src_ref=cs.at[f, yo], dst_ref=r2.at[f, 1], send_sem=s2.at[f, 1], recv_sem=q2.at[f, 1],
            device_id=(p, zd * 2 + yo), device_id_type=MESH).start()

    def head_copies():
        out = []
        for dz in (0, 1, -1, 2, -2, 3, -3, 4, -4, 5, -5, 6, -6, 7, -7, 8):
            for w, yy in enumerate((y, yo)):
                if dz == 0 and w == 0:
                    continue
                out.append(pltpu.make_async_remote_copy(
                    src_ref=rg.at[y], dst_ref=rg.at[y], send_sem=sg.at[len(out)], recv_sem=qg.at[y],
                    device_id=(p, at(dz, yy)), device_id_type=MESH))
        return out

    kt[...] = ka[...].T

    def query_grad(h, _):
        cols = pl.ds(pl.multiple_of(h * RESP, RESP), RESP)
        acc = jnp.dot(kt[...], ds_s[:, cols], preferred_element_type=F32)
        dq_out[0, 0, :, pl.ds(pl.multiple_of(h * DH, DH), DH)] = (acc * SCALE).T.astype(BF16)
        return 0

    lax.fori_loop(0, H, query_grad, 0)

    @pl.when(z == 0)
    def _():
        total = acc
        for i in range(1, NZ):
            arrived(rz.at[i], qz.at[i])
        for i in range(1, NZ):
            total = total + rz[i].astype(F32)
        rg[y] = total
        for i, c in enumerate(head_copies()):
            c.start()

    for f in range(3):
        for w in range(2):
            if f == 1 and w == 0:
                continue
            arrived(r2.at[f, w], q2.at[f, w])
    total = cs[1, y].astype(F32) + r2[1, 1].astype(F32)
    for f in (0, 2):
        for w in range(2):
            total = total + r2[f, w].astype(F32)
    tkg_out[0] = total[:32]
    tvg_out[0] = total[32:]

    arrived(rg.at[yo], qg.at[yo])

    @pl.when(z != 0)
    def _():
        arrived(rg.at[y], qg.at[y])

    for w in range(2):
        hkg_out[w * 16 : (w + 1) * 16, :] = rg[w, :16, :]
        hvg_out[w * 16 : (w + 1) * 16, :] = rg[w, 16:, :]

    for c in sent:
        c.wait_send()
    for zd in range(NZ):
        one, two, whole, low, high = near_copies(zd)

        @pl.when(one)
        def _():
            whole.wait_send()

        @pl.when(two)
        def _():
            low.wait_send()
            high.wait_send()

    for f in range(3):
        for w in range(2):
            if f == 1 and w == 0:
                continue
            pltpu.make_async_remote_copy(
                src_ref=cs.at[f, w], dst_ref=r2.at[f, w], send_sem=s2.at[f, w], recv_sem=q2.at[f, w],
                device_id=(p, at(1, y)), device_id_type=MESH).wait_send()

    @pl.when(z != 0)
    def _():
        pltpu.make_async_remote_copy(
            src_ref=zs, dst_ref=rz.at[z], send_sem=sz.at[0], recv_sem=qz.at[z],
            device_id=(p, y), device_id_type=MESH).wait_send()

    @pl.when(z == 0)
    def _():
        for c in head_copies():
            c.wait_send()


def finish_kernel(*refs):
    ins, outs, sem = refs[:7], refs[7:14], refs[14]
    copies = [pltpu.make_async_copy(a, o, sem.at[i]) for i, (a, o) in enumerate(zip(ins, outs))]
    for c in copies:
        c.start()
    for c in copies:
        c.wait()


def per_device(q, rk, rv, tk, tv, hk, hv, g, lengths, forks):
    vm = pl.BlockSpec(memory_space=pltpu.VMEM)
    hbm = pl.BlockSpec(memory_space=pltpu.HBM)
    dma = pltpu.SemaphoreType.DMA
    sds = jax.ShapeDtypeStruct
    V = pltpu.VMEM
    shapes = (
            sds((1, 1, RESP, H * DH), BF16), sds((1, 1, RESP, DH), BF16), sds((1, 1, RESP, DH), BF16),
            sds((1, 32, DH), F32), sds((1, 32, DH), F32), sds((32, DH), F32), sds((32, DH), F32),
    )
    args = [
        pltpu.with_memory_space_constraint(a, pltpu.HBM)
        for a in (q, rk, rv, tk, tv, hk, hv, g)]
    raw = pl.pallas_call(
        kernel,
        out_shape=shapes,
        in_specs=[hbm] * 10,
        out_specs=(vm,) * 7,
        scratch_shapes=[
            V((H * RESP, DH), BF16), V((H * RESP, DH), BF16),
            V((H, DH, RESP), BF16), V((H, DH, RESP), BF16),
            V((KEYS, DH), BF16), V((KEYS, DH), BF16), V((DH, KEYS), BF16),
            V((NP, 64, DH), BF16), V((NB, 64, DH), BF16),
            V((H, KEYS, RESP), F32), V((H, KEYS, RESP), F32), V((KEYS, H * RESP), BF16),
            V((H, 1, RESP), F32), V((H, 8, RESP), F32), V((H, 8, RESP), F32),
            V((NZ + 3, H, 1, RESP), F32), V((NZ + 3, H, 1, RESP), F32), V((H, 1, RESP), F32),
            V((NB, 64, DH), BF16), V((5, 3, 2, 64, DH), BF16),
            V((3, 2, 64, DH), BF16), V((3, 2, 64, DH), BF16),
            V((2 * NP, 32, DH), BF16), V((2 * NP, 32, DH), BF16),
            V((32, DH), BF16), V((NZ, 32, DH), BF16), V((2, 32, DH), F32),
            pltpu.SMEM((1, 1), jnp.int32), pltpu.SMEM((1, 1), jnp.int32),
            dma((4 + 2 * H,)), dma((4,)),
            dma((48,)), dma((NP,)), dma((NB,)), dma((2,)),
            dma((NZ + 1,)), dma((5, 3)),
            dma((3, 2)), dma((3, 2)),
            dma((31,)), dma((32,)), dma((1,)), dma((NZ,)), dma((31,)), dma((2,)),
        ],
        compiler_params=pltpu.CompilerParams(
            collective_id=0, has_side_effects=True, vmem_limit_bytes=52 << 20),
    )(lengths, forks, *args)
    return pl.pallas_call(
        finish_kernel,
        out_shape=shapes,
        in_specs=(vm,) * 7,
        out_specs=(hbm,) * 7,
        scratch_shapes=[dma((7,))],
    )(*raw)


def solution(mesh):
    four, three, two = P("prompt", "branch", None, None), P("prompt", "branch", None), P("prompt", None)
    both = P("prompt", "branch")
    return jax.shard_map(
        per_device,
        mesh=mesh,
        in_specs=(four, four, four, three, three, two, two, four, both, both),
        out_specs=(four, four, four, three, three, two, two),
        check_vma=False,
    )
```

time: 76.6 us -> 61.9 us (0.81)
  the two profiles are of different devices: /device:TPU:32 before, /device:TPU:1 now
where the time goes in v2:
time: 61.9 us; the launch traced here: 61.1 us
  Pallas kernels  54.8 us (89%)
  local copies, waits for them, and re-layouts  4.4 us (7%)
  between operations  1.95 us (3%)
    pallas_call x1, Pallas kernels, per_device(): pl.pallas_call(kernel, out_shape=shapes, in_specs=[hbm] * 10, out_specs=(...  52.7 us
    unnamed x14, local copies, waits for them, and re-layouts  4.4 us
    pallas_call x1, Pallas kernels, per_device(): pl.pallas_call(finish_kernel, out_shape=shapes, in_specs=(vm,) * 7, out_s...  2.02 us

profile of v2, /device:TPU:1, one launch (start us, length us, event | category | flops | bytes accessed | tf_op | source)
XLA Modules:
  0.0 61.1 jit_solution(7364437056313525058)
XLA Ops:
  1.9 52.7 %shard_map.153 = (bf16[1,1,256,1024]{3,2,1,0:T(8,128)(2,1)S(1)}, bf16[1,1,256,128]{3,2,1,0:T(8,128)(2,1)S(1)}, bf16[1,1,256,128]{3,2,1,0:T(8,128)(2,1)S(1)}, f32...) custom-call(s32[1,1]{1,0:T(1,128)S(6)} %copy.17.len_hbm, ...), custom_call_target="tpu_custom_call" | custom-call | tf_op jit(solution)/shard_map/pallas_call | solution.py:486
  54.7 0.0 copy-start
  54.7 0.8 %copy-done = bf16[1,1,256,1024]{3,2,1,0:T(8,128)(2,1)} copy-done((bf16[1,1,256,1024]{3,2,1,0:T(8,128)(2,1)}, bf16[1,1,256,1024]{3,2,1,0:T(8,128)(2,1)S(1)}, u32[]{:S(2)}) %copy-start) | copy-done | bytes 524312
  55.5 0.0 copy-start.1
  55.5 0.6 %copy-done.1 = bf16[1,1,256,128]{3,2,1,0:T(8,128)(2,1)} copy-done((bf16[1,1,256,128]{3,2,1,0:T(8,128)(2,1)}, bf16[1,1,256,128]{3,2,1,0:T(8,128)(2,1)S(1)}, u32[]{:S(2)}) %copy-start.1) | copy-done | bytes 65560
  56.1 0.0 copy-start.2
  56.1 0.6 %copy-done.2 = bf16[1,1,256,128]{3,2,1,0:T(8,128)(2,1)} copy-done((bf16[1,1,256,128]{3,2,1,0:T(8,128)(2,1)}, bf16[1,1,256,128]{3,2,1,0:T(8,128)(2,1)S(1)}, u32[]{:S(2)}) %copy-start.2) | copy-done | bytes 65560
  56.7 0.0 copy-start.3
  56.7 0.6 copy-done.3
  57.3 0.0 copy-start.4
  57.3 0.6 copy-done.4
  57.9 0.0 copy-start.5
  57.9 0.6 copy-done.5
  58.5 0.0 copy-start.6
  58.5 0.6 copy-done.6
  59.1 2.0 %shard_map.154 = (bf16[1,1,256,1024]{3,2,1,0:T(8,128)(2,1)}, bf16[1,1,256,128]{3,2,1,0:T(8,128)(2,1)}, bf16[1,1,256,128]{3,2,1,0:T(8,128)(2,1)}, f32[1,32,128]{2...) custom-call(bf16[1,1,256,1024]{3,2,1,0:T(8,128)(2,1)} %copy-done, ...), custom_call_target="tpu_custom_call" | custom-call | tf_op jit(solution)/shard_map/pallas_call | solution.py:513
Async XLA Ops:
  54.7 0.8 %copy-start = (bf16[1,1,256,1024]{3,2,1,0:T(8,128)(2,1)}, bf16[1,1,256,1024]{3,2,1,0:T(8,128)(2,1)S(1)}, u32[]{:S(2)}) copy-start(bf16[1,1,256,1024]{3,2,1,0:T(8,128)(2,1)S(1)} %get-tuple-element.14.refs_0_) | copy-start | bytes 1572868
  55.5 0.6 %copy-start.1 = (bf16[1,1,256,128]{3,2,1,0:T(8,128)(2,1)}, bf16[1,1,256,128]{3,2,1,0:T(8,128)(2,1)S(1)}, u32[]{:S(2)}) copy-start(bf16[1,1,256,128]{3,2,1,0:T(8,128)(2,1)S(1)} %get-tuple-element.15.refs_1_) | copy-start | bytes 196612
  56.1 0.6 %copy-start.2 = (bf16[1,1,256,128]{3,2,1,0:T(8,128)(2,1)}, bf16[1,1,256,128]{3,2,1,0:T(8,128)(2,1)S(1)}, u32[]{:S(2)}) copy-start(bf16[1,1,256,128]{3,2,1,0:T(8,128)(2,1)S(1)} %get-tuple-element.16.refs_2_) | copy-start | bytes 196612
  56.7 0.6 copy-start.3
  57.3 0.6 copy-start.4
  57.9 0.6 copy-start.5
  58.5 0.6 copy-start.6

commit v3 on v2

--- a/solution.py
+++ b/solution.py
@@ -19,8 +19,15 @@
 CH = 256
 KEYS = HDR + PREF + RESP
 NCH = KEYS // CH
-FAR = 5
-NEAR = (-2, -1, 1, 2)
+GATHER_STEP, GATHER_FARS = 3, 2
+STEP, FARS = 5, 1
+NEAR_MAX = STEP // 2
+SPOKES = 2 * FARS + 1
+REST = NZ // 2 - FARS * STEP
+G_NEAR_MAX = GATHER_STEP // 2
+G_REST = NZ // 2 - GATHER_FARS * GATHER_STEP
+NEAR = tuple(j for j in range(-G_NEAR_MAX, G_NEAR_MAX + 1) if j != 0)
+FAR = tuple(k * GATHER_STEP for k in range(-GATHER_FARS, GATHER_FARS + 1) if k != 0)
 LOW = -1e30
 SCALE = DH**-0.5
 LOG2E = 1.4426950408889634
@@ -36,11 +43,11 @@
 
 
 def kernel(
-    len_hbm, fork_hbm, q_hbm, rk_hbm, rv_hbm, tk_hbm, tv_hbm, hk_hbm, hv_hbm, g_hbm,
+    lengths, forks, q_hbm, rk_hbm, rv_hbm, tk_hbm, tv_hbm, hk_hbm, hv_hbm, g_hbm,
     dq_out, rkg_out, rvg_out, tkg_out, tvg_out, hkg_out, hvg_out,
     qf, gf, qt, gt, ka, va, kt, hkv, tkv, e_s, dp_s, ds_s, m_s, l_s, d_s, mb_s, fac_s, del_s,
     tb, r1, cs, r2, hb, rh, zs, rz, rg,
-    lengths, forks, in_sem, own_sem, gs, hrs, trs, ars, s1, q1, s2, q2, sh, qh, sz, qz, sg, qg,
+    in_sem, own_sem, gs, hrs, trs, ars, s1, q1, s2, q2, sh, qh, sz, qz, sg, qg,
 ):
     p = lax.axis_index("prompt")
     b = lax.axis_index("branch")
@@ -51,14 +58,6 @@
 
     def at(dz, yy):
         return mod(z + dz, NZ) * 2 + yy
-
-    barrier = pltpu.get_barrier_semaphore()
-    greet = [(p, at(s * FAR, yy)) for s in (-1, 1) for yy in (y, yo)]
-    greet += [(p, at(j, yy)) for j in (-3, -2, -1, 1, 2, 3) for yy in (y, yo)]
-    greet += [(p, at(0, yo))]
-    greet += [(mod(p + o, NP), b) for o in range(1, NP)]
-    for d in greet:
-        pl.semaphore_signal(barrier, 1, device_id=d, device_id_type=MESH)
 
     own = [
         pltpu.make_async_copy(hk_hbm, hkv.at[p, pl.ds(0, 32)], own_sem.at[0]),
@@ -68,12 +67,18 @@
     ]
     for c in own:
         c.start()
+    barrier = pltpu.get_barrier_semaphore()
+    greet = [(p, at(k, y)) for k in FAR]
+    greet += [(p, at(j, yy)) for j in sorted({*NEAR, -G_REST, G_REST}) for yy in (y, yo)]
+    greet += [(p, at(0, yo))]
+    greet += [(mod(p + o, NP), b) for o in range(1, NP)]
+    for d in greet:
+        pl.semaphore_signal(barrier, 1, device_id=d, device_id_type=MESH)
+
     loads = [
         pltpu.make_async_copy(rk_hbm.at[0, 0], ka.at[pl.ds(HDR + PREF, RESP)], in_sem.at[0]),
         pltpu.make_async_copy(rv_hbm.at[0, 0], va.at[pl.ds(HDR + PREF, RESP)], in_sem.at[1]),
     ]
-    loads.append(pltpu.make_async_copy(len_hbm, lengths, in_sem.at[2 + 2 * H]))
-    loads.append(pltpu.make_async_copy(fork_hbm, forks, in_sem.at[3 + 2 * H]))
     for h in range(H):
         loads.append(pltpu.make_async_copy(
             q_hbm.at[0, 0, :, pl.ds(h * DH, DH)], qf.at[pl.ds(h * RESP, RESP)], in_sem.at[2 + h]))
@@ -95,9 +100,9 @@
         sent.append(c)
 
     n = 0
-    slots = [b, at(-FAR, y), at(FAR, y)]
-    for s in (-1, 1):
-        send(tkv.at[b], tkv.at[b], gs.at[n], trs.at[b], (p, at(s * FAR, y)))
+    slots = [b] + [at(k, y) for k in FAR]
+    for k in sorted(FAR, key=abs, reverse=True):
+        send(tkv.at[b], tkv.at[b], gs.at[n], trs.at[b], (p, at(k, y)))
         n += 1
     near = [at(j, yy) for j in NEAR for yy in (y, yo)] + [at(0, yo)]
     for d in near:
@@ -123,9 +128,10 @@
         return 0
 
     lax.fori_loop(0, H, prepare, 0)
-    r1[4, 0, :, :32, :] = jnp.zeros((2, 32, DH), BF16)
-    r1[4, 1] = jnp.zeros((2, 64, DH), BF16)
-    r1[4, 2, :, 32:, :] = jnp.zeros((2, 32, DH), BF16)
+    r1[2 * NEAR_MAX, 0, :, :32, :] = jnp.zeros((2, 32, DH), BF16)
+    for f in range(1, 2 * FARS):
+        r1[2 * NEAR_MAX, f] = jnp.zeros((2, 64, DH), BF16)
+    r1[2 * NEAR_MAX, 2 * FARS, :, 32:, :] = jnp.zeros((2, 32, DH), BF16)
     fork = forks[0, 0]
 
     def stats(h, spots, seen, kind):
@@ -185,25 +191,24 @@
 
     stats_of([(HDR + PREF, RESP)], [None], "resp", [NZ + 2])
 
-    for s in slots[1:]:
-        pltpu.make_async_remote_copy(
-            src_ref=tkv.at[s], dst_ref=tkv.at[s], send_sem=gs.at[0], recv_sem=trs.at[s],
-            device_id=(p, at(1, y)), device_id_type=MESH).wait_recv()
-    for s in slots[1:]:
-        for d in near:
-            send(tkv.at[s], tkv.at[s], gs.at[n], trs.at[s], (p, d))
-            n += 1
-    kk, vv = pl.ds(0, 32), pl.ds(32, 32)
-    for yy in (y, yo):
-        send(tkv.at[slots[1], kk], tkv.at[slots[1], kk], gs.at[n], trs.at[slots[1]], (p, at(3, yy)))
-        n += 1
-        send(tkv.at[slots[2], vv], tkv.at[slots[2], vv], gs.at[n], ars.at[lax.rem(slots[2], 2)], (p, at(-3, yy)))
-        n += 1
-
     def arrived(ref, sem):
         pltpu.make_async_remote_copy(
             src_ref=ref, dst_ref=ref, send_sem=gs.at[0], recv_sem=sem,
             device_id=(p, at(1, y)), device_id_type=MESH).wait_recv()
+
+    kk, vv = pl.ds(0, 32), pl.ds(32, 32)
+    for k in sorted(FAR, key=abs):
+        s = at(k, y)
+        arrived(tkv.at[s], trs.at[s])
+        for d in near:
+            send(tkv.at[s], tkv.at[s], gs.at[n], trs.at[s], (p, d))
+            n += 1
+    first, last = at(FAR[0], y), at(FAR[-1], y)
+    for yy in (y, yo):
+        send(tkv.at[first, kk], tkv.at[first, kk], gs.at[n], trs.at[first], (p, at(G_REST, yy)))
+        n += 1
+        send(tkv.at[last, vv], tkv.at[last, vv], gs.at[n], ars.at[y], (p, at(-G_REST, yy)))
+        n += 1
 
     for o in range(1, NP):
         s = mod(p + o, NP)
@@ -219,7 +224,7 @@
     lax.fori_loop(0, HDR // CH, head_stats, 0)
 
     def group(j):
-        return [mod(z + j + f * FAR, NZ) for f in (0, -1, 1)]
+        return [mod(z + j + k, NZ) for k in sorted((0, *FAR), key=abs)]
 
     for zb in group(0):
         arrived(tkv.at[2 * zb + yo], trs.at[2 * zb + yo])
@@ -233,7 +238,7 @@
         trunk_stats(group(j))
         return 0
 
-    lax.fori_loop(1, 5, near_group, 0)
+    lax.fori_loop(1, 2 * G_NEAR_MAX + 1, near_group, 0)
     anti = mod(z + 8, NZ)
     for yy in (y, yo):
         arrived(tkv.at[2 * anti + yy, kk], trs.at[2 * anti + yy])
@@ -264,6 +269,11 @@
             vg = vg + jnp.dot(pr.astype(BF16), gf[h * RESP : (h + 1) * RESP, :], preferred_element_type=F32)
         return kg * SCALE, vg
 
+    def head_copy(q):
+        return pltpu.make_async_remote_copy(
+            src_ref=hb.at[q], dst_ref=rh.at[plane], send_sem=sh.at[q], recv_sem=qh.at[plane],
+            device_id=(q // 2, z * 2 + lax.rem(q, 2)), device_id_type=MESH)
+
     def head_terms(i, _):
         kg, vg = terms(pl.multiple_of(i * CH, CH), [NZ + i])
         kg, vg = kg.astype(BF16), vg.astype(BF16)
@@ -273,33 +283,32 @@
         return 0
 
     lax.fori_loop(0, HDR // CH, head_terms, 0)
-
-    n = 0
     for o in range(1, 2 * NP):
-        d = mod(plane + o, 2 * NP)
-        send(hb.at[d], rh.at[plane], sh.at[n], qh.at[plane], (d // 2, z * 2 + lax.rem(d, 2)))
-        n += 1
+        head_copy(mod(plane + o, 2 * NP)).start()
 
     def route(zd):
         o = mod(zd - z, NZ)
-        near_it = jnp.logical_or(o <= 2, o >= NZ - 2)
-        f = jnp.where(near_it, 1, jnp.where(o <= 8, 2, 0))
-        j = jnp.where(o <= 2, o, jnp.where(o <= 8, o - FAR, jnp.where(o <= 13, o - 11, o - NZ)))
-        jn = jnp.where(o == 8, 4, jnp.where(j < 0, j + 2, j + 1))
-        return o, j, jn, f
+        signed = jnp.where(o > NZ // 2, o - NZ, o)
+        f = (signed + NEAR_MAX + FARS * STEP) // STEP
+        j = signed - (f - FARS) * STEP
+        jn = jnp.where(j < 0, j + NEAR_MAX, j + NEAR_MAX - 1)
+        ok = jnp.logical_and(o != NZ // 2, j != 0)
+        return o, ok, jnp.where(ok, j, 1), jnp.where(ok, jn, 0), jnp.where(ok, f, 0)
 
     def near_copies(zd):
-        o, j, jn, f = route(zd)
+        o, ok, j, jn, f = route(zd)
         whole = pltpu.make_async_remote_copy(
             src_ref=tb.at[pl.ds(2 * zd, 2)], dst_ref=r1.at[jn, f], send_sem=s1.at[zd], recv_sem=q1.at[jn, f],
             device_id=(p, mod(z + j, NZ) * 2 + y), device_id_type=MESH)
         low = pltpu.make_async_remote_copy(
-            src_ref=tb.at[pl.ds(2 * zd, 2), kk], dst_ref=r1.at[4, 2, :, kk], send_sem=s1.at[zd], recv_sem=q1.at[4, 2],
-            device_id=(p, at(3, y)), device_id_type=MESH)
+            src_ref=tb.at[pl.ds(2 * zd, 2), kk], dst_ref=r1.at[2 * NEAR_MAX, 2 * FARS, :, kk],
+            send_sem=s1.at[zd], recv_sem=q1.at[2 * NEAR_MAX, 2 * FARS],
+            device_id=(p, at(REST, y)), device_id_type=MESH)
         high = pltpu.make_async_remote_copy(
-            src_ref=tb.at[pl.ds(2 * zd, 2), vv], dst_ref=r1.at[4, 0, :, vv], send_sem=s1.at[NZ], recv_sem=q1.at[4, 0],
-            device_id=(p, at(-3, y)), device_id_type=MESH)
-        return jnp.logical_and(o != 8, j != 0), o == 8, whole, low, high
+            src_ref=tb.at[pl.ds(2 * zd, 2), vv], dst_ref=r1.at[2 * NEAR_MAX, 0, :, vv],
+            send_sem=s1.at[NZ], recv_sem=q1.at[2 * NEAR_MAX, 0],
+            device_id=(p, at(-REST, y)), device_id_type=MESH)
+        return ok, o == NZ // 2, whole, low, high
 
     def trunk_terms(i, _):
         kg, vg = terms(pl.multiple_of(HDR + i * CH, CH), [i * 4 + u for u in range(4)])
@@ -342,28 +351,28 @@
             src_ref=zs, dst_ref=rz.at[z], send_sem=sz.at[0], recv_sem=qz.at[z],
             device_id=(p, y), device_id_type=MESH).start()
 
-    dests = [mod(z + (f - 1) * FAR, NZ) for f in range(3)]
+    dests = [mod(z + (f - FARS) * STEP, NZ) for f in range(SPOKES)]
     ranks = [sum((other < d).astype(jnp.int32) for other in dests) for d in dests]
-    for k in range(3):
+    for k in range(SPOKES):
         f = sum(jnp.where(r == k, i, 0) for i, r in enumerate(ranks))
-        zd = mod(z + (f - 1) * FAR, NZ)
-        for jn in range(4):
+        zd = mod(z + (f - FARS) * STEP, NZ)
+        for jn in range(2 * NEAR_MAX):
             arrived(r1.at[jn, f], q1.at[jn, f])
 
         @pl.when(f == 0)
         def _():
-            arrived(r1.at[4, 0, :, vv], q1.at[4, 0])
-
-        @pl.when(f == 2)
+            arrived(r1.at[2 * NEAR_MAX, 0, :, vv], q1.at[2 * NEAR_MAX, 0])
+
+        @pl.when(f == 2 * FARS)
         def _():
-            arrived(r1.at[4, 2, :, kk], q1.at[4, 2])
+            arrived(r1.at[2 * NEAR_MAX, 2 * FARS, :, kk], q1.at[2 * NEAR_MAX, 2 * FARS])
 
         total = tb[pl.ds(2 * zd, 2)].astype(F32)
-        for jn in range(5):
+        for jn in range(2 * NEAR_MAX + 1):
             total = total + r1[jn, f].astype(F32)
         cs[f] = total.astype(BF16)
 
-        @pl.when(f != 1)
+        @pl.when(f != FARS)
         def _():
             pltpu.make_async_remote_copy(
                 src_ref=cs.at[f, y], dst_ref=r2.at[f, 0], send_sem=s2.at[f, 0], recv_sem=q2.at[f, 0],
@@ -394,6 +403,26 @@
 
     lax.fori_loop(0, H, query_grad, 0)
 
+    for c in sent:
+        c.wait_send()
+    for zd in range(NZ):
+        one, two, whole, low, high = near_copies(zd)
+
+        @pl.when(one)
+        def _():
+            whole.wait_send()
+
+        @pl.when(two)
+        def _():
+            low.wait_send()
+            high.wait_send()
+
+    for q in range(2 * NP):
+
+        @pl.when(q != plane)
+        def _():
+            head_copy(q).wait_send()
+
     @pl.when(z == 0)
     def _():
         total = acc
@@ -401,19 +430,16 @@
             arrived(rz.at[i], qz.at[i])
         for i in range(1, NZ):
             total = total + rz[i].astype(F32)
-        rg[y] = total
+        rg[y] = total.astype(BF16)
         for i, c in enumerate(head_copies()):
             c.start()
 
-    for f in range(3):
-        for w in range(2):
-            if f == 1 and w == 0:
-                continue
-            arrived(r2.at[f, w], q2.at[f, w])
-    total = cs[1, y].astype(F32) + r2[1, 1].astype(F32)
-    for f in (0, 2):
-        for w in range(2):
-            total = total + r2[f, w].astype(F32)
+    spokes = [(f, w) for f in range(SPOKES) for w in range(2) if (f, w) != (FARS, 0)]
+    for f, w in spokes:
+        arrived(r2.at[f, w], q2.at[f, w])
+    total = cs[FARS, y].astype(F32)
+    for f, w in spokes:
+        total = total + r2[f, w].astype(F32)
     tkg_out[0] = total[:32]
     tvg_out[0] = total[32:]
 
@@ -424,31 +450,13 @@
         arrived(rg.at[y], qg.at[y])
 
     for w in range(2):
-        hkg_out[w * 16 : (w + 1) * 16, :] = rg[w, :16, :]
-        hvg_out[w * 16 : (w + 1) * 16, :] = rg[w, 16:, :]
-
-    for c in sent:
-        c.wait_send()
-    for zd in range(NZ):
-        one, two, whole, low, high = near_copies(zd)
-
-        @pl.when(one)
-        def _():
-            whole.wait_send()
-
-        @pl.when(two)
-        def _():
-            low.wait_send()
-            high.wait_send()
-
-    for f in range(3):
-        for w in range(2):
-            if f == 1 and w == 0:
-                continue
-            pltpu.make_async_remote_copy(
-                src_ref=cs.at[f, w], dst_ref=r2.at[f, w], send_sem=s2.at[f, w], recv_sem=q2.at[f, w],
-                device_id=(p, at(1, y)), device_id_type=MESH).wait_send()
-
+        hkg_out[w * 16 : (w + 1) * 16, :] = rg[w, :16, :].astype(F32)
+        hvg_out[w * 16 : (w + 1) * 16, :] = rg[w, 16:, :].astype(F32)
+
+    for f, w in spokes:
+        pltpu.make_async_remote_copy(
+            src_ref=cs.at[f, w], dst_ref=r2.at[f, w], send_sem=s2.at[f, w], recv_sem=q2.at[f, w],
+            device_id=(p, at(1, y)), device_id_type=MESH).wait_send()
     @pl.when(z != 0)
     def _():
         pltpu.make_async_remote_copy(
@@ -473,6 +481,7 @@
 def per_device(q, rk, rv, tk, tv, hk, hv, g, lengths, forks):
     vm = pl.BlockSpec(memory_space=pltpu.VMEM)
     hbm = pl.BlockSpec(memory_space=pltpu.HBM)
+    smem = pl.BlockSpec(memory_space=pltpu.SMEM)
     dma = pltpu.SemaphoreType.DMA
     sds = jax.ShapeDtypeStruct
     V = pltpu.VMEM
@@ -486,7 +495,7 @@
     raw = pl.pallas_call(
         kernel,
         out_shape=shapes,
-        in_specs=[hbm] * 10,
+        in_specs=[smem, smem] + [hbm] * 8,
         out_specs=(vm,) * 7,
         scratch_shapes=[
             V((H * RESP, DH), BF16), V((H * RESP, DH), BF16),
@@ -496,16 +505,15 @@
             V((H, KEYS, RESP), F32), V((H, KEYS, RESP), F32), V((KEYS, H * RESP), BF16),
             V((H, 1, RESP), F32), V((H, 8, RESP), F32), V((H, 8, RESP), F32),
             V((NZ + 3, H, 1, RESP), F32), V((NZ + 3, H, 1, RESP), F32), V((H, 1, RESP), F32),
-            V((NB, 64, DH), BF16), V((5, 3, 2, 64, DH), BF16),
-            V((3, 2, 64, DH), BF16), V((3, 2, 64, DH), BF16),
+            V((NB, 64, DH), BF16), V((2 * NEAR_MAX + 1, SPOKES, 2, 64, DH), BF16),
+            V((SPOKES, 2, 64, DH), BF16), V((SPOKES, 2, 64, DH), BF16),
             V((2 * NP, 32, DH), BF16), V((2 * NP, 32, DH), BF16),
-            V((32, DH), BF16), V((NZ, 32, DH), BF16), V((2, 32, DH), F32),
-            pltpu.SMEM((1, 1), jnp.int32), pltpu.SMEM((1, 1), jnp.int32),
-            dma((4 + 2 * H,)), dma((4,)),
+            V((32, DH), BF16), V((NZ, 32, DH), BF16), V((2, 32, DH), BF16),
+            dma((2 + 2 * H,)), dma((4,)),
             dma((48,)), dma((NP,)), dma((NB,)), dma((2,)),
-            dma((NZ + 1,)), dma((5, 3)),
-            dma((3, 2)), dma((3, 2)),
-            dma((31,)), dma((32,)), dma((1,)), dma((NZ,)), dma((31,)), dma((2,)),
+            dma((NZ + 1,)), dma((2 * NEAR_MAX + 1, SPOKES)),
+            dma((SPOKES, 2)), dma((SPOKES, 2)),
+            dma((32,)), dma((32,)), dma((1,)), dma((NZ,)), dma((31,)), dma((2,)),
         ],
         compiler_params=pltpu.CompilerParams(
             collective_id=0, has_side_effects=True, vmem_limit_bytes=52 << 20),
@@ -516,7 +524,7 @@
         in_specs=(vm,) * 7,
         out_specs=(hbm,) * 7,
         scratch_shapes=[dma((7,))],
-    )(*raw)
+    )(*[pltpu.with_memory_space_constraint(a, pltpu.VMEM) for a in raw])
 
 
 def solution(mesh):

time: 61.9 us -> 55.1 us (0.89)
  local copies, waits for them, and re-layouts: 4.4 us -> 0 us
  Pallas kernels: 54.8 us -> 52.2 us
    unnamed x14 -> x0, local copies, waits for them, and re-layouts: 4.4 us -> none
    pallas_call x1, Pallas kernels: 52.7 us -> 51.3 us  [per_device(): pl.pallas_call(kernel, out_shape=shapes, in_specs=[smem, smem] + [hbm] *...]
    pallas_call x1, Pallas kernels: 2.02 us -> 0.9 us  [per_device(): pl.pallas_call(finish_kernel, out_shape=shapes, in_specs=(vm,) * 7, out_s...]
where the time goes in v3:
time: 55.1 us; the launch traced here: 54.1 us
  Pallas kernels  52.2 us (95%)
  between operations  1.94 us (4%)
    pallas_call x1, Pallas kernels, per_device(): pl.pallas_call(kernel, out_shape=shapes, in_specs=[smem, smem] + [hbm] *...  51.3 us

profile of v3, /device:TPU:1, one launch (start us, length us, event | category | flops | bytes accessed | tf_op | source)
XLA Modules:
  0.0 54.1 jit_solution(12970471080762891330)
XLA Ops:
  1.9 51.3 %shard_map.153 = (bf16[1,1,256,1024]{3,2,1,0:T(8,128)(2,1)S(1)}, bf16[1,1,256,128]{3,2,1,0:T(8,128)(2,1)S(1)}, bf16[1,1,256,128]{3,2,1,0:T(8,128)(2,1)S(1)}, f32...) custom-call(s32[1,1]{1,0:T(1,128)S(6)} %copy.17.lengths, ...), custom_call_target="tpu_custom_call" | custom-call | tf_op jit(solution)/shard_map/pallas_call | solution.py:495
  53.2 0.9 %shard_map.154 = (bf16[1,1,256,1024]{3,2,1,0:T(8,128)(2,1)}, bf16[1,1,256,128]{3,2,1,0:T(8,128)(2,1)}, bf16[1,1,256,128]{3,2,1,0:T(8,128)(2,1)}, f32[1,32,128]{2...) custom-call(bf16[1,1,256,1024]{3,2,1,0:T(8,128)(2,1)S(1)} %get-tuple-element.14.refs_0_, ...), custom_call_target="tpu_custom_call" | custom-call | tf_op jit(solution)/shard_map/pallas_call | solution.py:521

commit v4 on v3

--- a/solution.py
+++ b/solution.py
@@ -197,12 +197,29 @@
             device_id=(p, at(1, y)), device_id_type=MESH).wait_recv()
 
     kk, vv = pl.ds(0, 32), pl.ds(32, 32)
-    for k in sorted(FAR, key=abs):
+    def pass_on(k, n):
         s = at(k, y)
         arrived(tkv.at[s], trs.at[s])
         for d in near:
             send(tkv.at[s], tkv.at[s], gs.at[n], trs.at[s], (p, d))
             n += 1
+        return n
+
+    def group(k):
+        for yy in (y, yo):
+            for j in NEAR:
+                arrived(tkv.at[at(k + j, yy)], trs.at[at(k + j, yy)])
+        arrived(tkv.at[at(k, yo)], trs.at[at(k, yo)])
+        return [mod(z + k + j, NZ) for j in (0, *NEAR)]
+
+    by_distance = sorted(FAR, key=abs)
+    for k in by_distance:
+        if abs(k) == GATHER_STEP:
+            n = pass_on(k, n)
+    trunk_stats(group(0))
+    for k in by_distance:
+        if abs(k) > GATHER_STEP:
+            n = pass_on(k, n)
     first, last = at(FAR[0], y), at(FAR[-1], y)
     for yy in (y, yo):
         send(tkv.at[first, kk], tkv.at[first, kk], gs.at[n], trs.at[first], (p, at(G_REST, yy)))
@@ -223,27 +240,18 @@
 
     lax.fori_loop(0, HDR // CH, head_stats, 0)
 
-    def group(j):
-        return [mod(z + j + k, NZ) for k in sorted((0, *FAR), key=abs)]
-
-    for zb in group(0):
-        arrived(tkv.at[2 * zb + yo], trs.at[2 * zb + yo])
-    trunk_stats(group(0))
-
-    def near_group(k, _):
-        j = ((k + 1) // 2) * (2 * lax.rem(k, 2) - 1)
-        for zb in group(j):
-            for yy in (y, yo):
-                arrived(tkv.at[2 * zb + yy], trs.at[2 * zb + yy])
-        trunk_stats(group(j))
-        return 0
-
-    lax.fori_loop(1, 2 * G_NEAR_MAX + 1, near_group, 0)
+    def far_group(i, _):
+        k = (i // 2 + 1) * GATHER_STEP * (1 - 2 * lax.rem(i, 2))
+        trunk_stats(group(k))
+        return 0
+
+    lax.fori_loop(0, 2 * GATHER_FARS - 1, far_group, 0)
+    last_group = group(-GATHER_FARS * GATHER_STEP)
     anti = mod(z + 8, NZ)
     for yy in (y, yo):
         arrived(tkv.at[2 * anti + yy, kk], trs.at[2 * anti + yy])
         arrived(tkv.at[2 * anti + yy, vv], ars.at[yy])
-    trunk_stats([anti])
+    trunk_stats(last_group + [anti])
 
     def finish(h, _):
         inv = 1.0 / jnp.sum(l_s[h], axis=0, keepdims=True)
@@ -253,7 +261,7 @@
             fac_s[i, h] = jnp.exp2((mb_s[i, h] - m) * C2) * inv
         return 0
 
-    lax.fori_loop(0, H, finish, 0)
+    lax.fori_loop(0, H, finish, 0, unroll=UNROLL)
 
     def terms(first, marks):
         rows = pl.ds(first, CH)
@@ -332,10 +340,6 @@
 
     lax.fori_loop(0, PREF // CH, trunk_terms, 0)
 
-    kg, vg = terms(HDR + PREF, [NZ + 2])
-    rkg_out[0, 0] = kg.astype(BF16)
-    rvg_out[0, 0] = vg.astype(BF16)
-
     for o in range(1, 2 * NP):
         s = mod(plane + o, 2 * NP)
         arrived(rh.at[s], qh.at[s])
@@ -350,6 +354,20 @@
         pltpu.make_async_remote_copy(
             src_ref=zs, dst_ref=rz.at[z], send_sem=sz.at[0], recv_sem=qz.at[z],
             device_id=(p, y), device_id_type=MESH).start()
+
+    kg, vg = terms(HDR + PREF, [NZ + 2])
+    rkg_out[0, 0] = kg.astype(BF16)
+    rvg_out[0, 0] = vg.astype(BF16)
+
+    kt[...] = ka[...].T
+
+    def query_grad(h, _):
+        cols = pl.ds(pl.multiple_of(h * RESP, RESP), RESP)
+        acc = jnp.dot(kt[...], ds_s[:, cols], preferred_element_type=F32)
+        dq_out[0, 0, :, pl.ds(pl.multiple_of(h * DH, DH), DH)] = (acc * SCALE).T.astype(BF16)
+        return 0
+
+    lax.fori_loop(0, H // 2, query_grad, 0)
 
     dests = [mod(z + (f - FARS) * STEP, NZ) for f in range(SPOKES)]
     ranks = [sum((other < d).astype(jnp.int32) for other in dests) for d in dests]
@@ -393,35 +411,7 @@
                     device_id=(p, at(dz, yy)), device_id_type=MESH))
         return out
 
-    kt[...] = ka[...].T
-
-    def query_grad(h, _):
-        cols = pl.ds(pl.multiple_of(h * RESP, RESP), RESP)
-        acc = jnp.dot(kt[...], ds_s[:, cols], preferred_element_type=F32)
-        dq_out[0, 0, :, pl.ds(pl.multiple_of(h * DH, DH), DH)] = (acc * SCALE).T.astype(BF16)
-        return 0
-
-    lax.fori_loop(0, H, query_grad, 0)
-
-    for c in sent:
-        c.wait_send()
-    for zd in range(NZ):
-        one, two, whole, low, high = near_copies(zd)
-
-        @pl.when(one)
-        def _():
-            whole.wait_send()
-
-        @pl.when(two)
-        def _():
-            low.wait_send()
-            high.wait_send()
-
-    for q in range(2 * NP):
-
-        @pl.when(q != plane)
-        def _():
-            head_copy(q).wait_send()
+    lax.fori_loop(H // 2, H, query_grad, 0)
 
     @pl.when(z == 0)
     def _():
@@ -433,6 +423,26 @@
         rg[y] = total.astype(BF16)
         for i, c in enumerate(head_copies()):
             c.start()
+
+    for c in sent:
+        c.wait_send()
+    for zd in range(NZ):
+        one, two, whole, low, high = near_copies(zd)
+
+        @pl.when(one)
+        def _():
+            whole.wait_send()
+
+        @pl.when(two)
+        def _():
+            low.wait_send()
+            high.wait_send()
+
+    for q in range(2 * NP):
+
+        @pl.when(q != plane)
+        def _():
+            head_copy(q).wait_send()
 
     spokes = [(f, w) for f in range(SPOKES) for w in range(2) if (f, w) != (FARS, 0)]
     for f, w in spokes:

time: 55.1 us -> 53 us (0.962); the launches traced: 54.1 us -> 52.7 us
  Pallas kernels: 52.2 us -> 50.8 us
    pallas_call x1, Pallas kernels: 51.3 us -> 49.9 us  [per_device(): pl.pallas_call(kernel, out_shape=shapes, in_specs=[smem, smem] + [hbm] *...]
where the time goes in v4:
time: 53 us; the launch traced here: 52.7 us
  Pallas kernels  50.8 us (96%)
  between operations  1.94 us (4%)
    pallas_call x1, Pallas kernels, per_device(): pl.pallas_call(kernel, out_shape=shapes, in_specs=[smem, smem] + [hbm] *...  49.9 us

profile of v4, /device:TPU:1, one launch (start us, length us, event | category | flops | bytes accessed | tf_op | source)
XLA Modules:
  0.0 52.7 jit_solution(17026332143430580295)
XLA Ops:
  1.9 49.9 %shard_map.153 = (bf16[1,1,256,1024]{3,2,1,0:T(8,128)(2,1)S(1)}, bf16[1,1,256,128]{3,2,1,0:T(8,128)(2,1)S(1)}, bf16[1,1,256,128]{3,2,1,0:T(8,128)(2,1)S(1)}, f32...) custom-call(s32[1,1]{1,0:T(1,128)S(6)} %copy.17.lengths, ...), custom_call_target="tpu_custom_call" | custom-call | tf_op jit(solution)/shard_map/pallas_call | solution.py:505
  51.8 0.9 %shard_map.154 = (bf16[1,1,256,1024]{3,2,1,0:T(8,128)(2,1)}, bf16[1,1,256,128]{3,2,1,0:T(8,128)(2,1)}, bf16[1,1,256,128]{3,2,1,0:T(8,128)(2,1)}, f32[1,32,128]{2...) custom-call(bf16[1,1,256,1024]{3,2,1,0:T(8,128)(2,1)S(1)} %get-tuple-element.14.refs_0_, ...), custom_call_target="tpu_custom_call" | custom-call | tf_op jit(solution)/shard_map/pallas_call | solution.py:531

commit v5 on v4

--- a/solution.py
+++ b/solution.py
@@ -45,7 +45,7 @@
 def kernel(
     lengths, forks, q_hbm, rk_hbm, rv_hbm, tk_hbm, tv_hbm, hk_hbm, hv_hbm, g_hbm,
     dq_out, rkg_out, rvg_out, tkg_out, tvg_out, hkg_out, hvg_out,
-    qf, gf, qt, gt, ka, va, kt, hkv, tkv, e_s, dp_s, ds_s, m_s, l_s, d_s, mb_s, fac_s, del_s,
+    qf, gf, qt, gt, ka, va, kt, hkv, tkv, e_s, dp_s, ds_s, m_s, l_s, d_s, mb_s, fac_s, del_s, inv_s,
     tb, r1, cs, r2, hb, rh, zs, rz, rg,
     in_sem, own_sem, gs, hrs, trs, ars, s1, q1, s2, q2, sh, qh, sz, qz, sg, qg,
 ):
@@ -245,8 +245,8 @@
         trunk_stats(group(k))
         return 0
 
-    lax.fori_loop(0, 2 * GATHER_FARS - 1, far_group, 0)
-    last_group = group(-GATHER_FARS * GATHER_STEP)
+    lax.fori_loop(0, 2 * GATHER_FARS - 2, far_group, 0)
+    last_group = group(GATHER_FARS * GATHER_STEP) + group(-GATHER_FARS * GATHER_STEP)
     anti = mod(z + 8, NZ)
     for yy in (y, yo):
         arrived(tkv.at[2 * anti + yy, kk], trs.at[2 * anti + yy])
@@ -257,11 +257,17 @@
         inv = 1.0 / jnp.sum(l_s[h], axis=0, keepdims=True)
         del_s[h] = jnp.sum(d_s[h], axis=0, keepdims=True) * inv
         m = m_s[h]
-        for i in range(NZ + 3):
+        inv_s[h] = inv
+        for i in range(NZ, NZ + 3):
             fac_s[i, h] = jnp.exp2((mb_s[i, h] - m) * C2) * inv
         return 0
 
     lax.fori_loop(0, H, finish, 0, unroll=UNROLL)
+
+    def finish_trunk(h, _):
+        for i in range(NZ):
+            fac_s[i, h] = jnp.exp2((mb_s[i, h] - m_s[h]) * C2) * inv_s[h]
+        return 0
 
     def terms(first, marks):
         rows = pl.ds(first, CH)
@@ -338,15 +344,14 @@
                 high.start()
         return 0
 
+    lax.fori_loop(0, H, finish_trunk, 0, unroll=UNROLL)
     lax.fori_loop(0, PREF // CH, trunk_terms, 0)
 
+    acc = hb[plane].astype(F32)
     for o in range(1, 2 * NP):
         s = mod(plane + o, 2 * NP)
         arrived(rh.at[s], qh.at[s])
-    rh[plane] = hb[plane]
-    acc = jnp.zeros((32, DH), F32)
-    for i in range(2 * NP):
-        acc = acc + rh[i].astype(F32)
+        acc = acc + rh[s].astype(F32)
     zs[...] = acc.astype(BF16)
 
     @pl.when(z != 0)
@@ -416,9 +421,8 @@
     @pl.when(z == 0)
     def _():
         total = acc
-        for i in range(1, NZ):
+        for i in sorted(range(1, NZ), key=lambda i: min(i, NZ - i)):
             arrived(rz.at[i], qz.at[i])
-        for i in range(1, NZ):
             total = total + rz[i].astype(F32)
         rg[y] = total.astype(BF16)
         for i, c in enumerate(head_copies()):
@@ -514,7 +518,7 @@
             V((NP, 64, DH), BF16), V((NB, 64, DH), BF16),
             V((H, KEYS, RESP), F32), V((H, KEYS, RESP), F32), V((KEYS, H * RESP), BF16),
             V((H, 1, RESP), F32), V((H, 8, RESP), F32), V((H, 8, RESP), F32),
-            V((NZ + 3, H, 1, RESP), F32), V((NZ + 3, H, 1, RESP), F32), V((H, 1, RESP), F32),
+            V((NZ + 3, H, 1, RESP), F32), V((NZ + 3, H, 1, RESP), F32), V((H, 1, RESP), F32), V((H, 1, RESP), F32),
             V((NB, 64, DH), BF16), V((2 * NEAR_MAX + 1, SPOKES, 2, 64, DH), BF16),
             V((SPOKES, 2, 64, DH), BF16), V((SPOKES, 2, 64, DH), BF16),
             V((2 * NP, 32, DH), BF16), V((2 * NP, 32, DH), BF16),

time: 53 us -> 55 us (1.038)
  Pallas kernels: 50.8 us -> 52.8 us
    pallas_call x1, Pallas kernels: 49.9 us -> 51.9 us  [per_device(): pl.pallas_call(kernel, out_shape=shapes, in_specs=[smem, smem] + [hbm] *...]
where the time goes in v5:
time: 55 us; the launch traced here: 54.8 us
  Pallas kernels  52.8 us (96%)
  between operations  1.94 us (4%)
    pallas_call x1, Pallas kernels, per_device(): pl.pallas_call(kernel, out_shape=shapes, in_specs=[smem, smem] + [hbm] *...  51.9 us

profile of v5, /device:TPU:1, one launch (start us, length us, event | category | flops | bytes accessed | tf_op | source)
XLA Modules:
  0.0 54.8 jit_solution(9404067143522376989)
XLA Ops:
  1.9 51.9 %shard_map.153 = (bf16[1,1,256,1024]{3,2,1,0:T(8,128)(2,1)S(1)}, bf16[1,1,256,128]{3,2,1,0:T(8,128)(2,1)S(1)}, bf16[1,1,256,128]{3,2,1,0:T(8,128)(2,1)S(1)}, f32...) custom-call(s32[1,1]{1,0:T(1,128)S(6)} %copy.17.lengths, ...), custom_call_target="tpu_custom_call" | custom-call | tf_op jit(solution)/shard_map/pallas_call | solution.py:509
  53.9 0.9 %shard_map.154 = (bf16[1,1,256,1024]{3,2,1,0:T(8,128)(2,1)}, bf16[1,1,256,128]{3,2,1,0:T(8,128)(2,1)}, bf16[1,1,256,128]{3,2,1,0:T(8,128)(2,1)}, f32[1,32,128]{2...) custom-call(bf16[1,1,256,1024]{3,2,1,0:T(8,128)(2,1)S(1)} %get-tuple-element.14.refs_0_, ...), custom_call_target="tpu_custom_call" | custom-call | tf_op jit(solution)/shard_map/pallas_call | solution.py:535
